TPU v7x, 32 devices: a whole 2x2x4 slice. The times are simulated.
32 devices in a mesh: dp: 8 (over y, x, core), seq: 4 (over z).
Axes of the slice: x: 2, y: 2, z: 4, core: 2. Of those that a mesh axis runs over, the one named last changes fastest.
Arguments:
- tokens: bfloat16 [8, 1024, 2048], P('dp', 'seq'), may hold values from -6 to 6
- cotangent: bfloat16 [8, 1024, 2048], P('dp', 'seq'), may hold values from -6 to 6
- attend_in: float32 [1024, 2, 4096], P(('dp', 'seq')), may hold values from -0.1875 to 0.1875
- attend_out: float32 [1024, 2, 2048], P(('dp', 'seq')), may hold values from -0.25 to 0.25
- gate_up: float32 [1024, 2, 16384], P(('dp', 'seq')), may hold values from -0.125 to 0.125
- down_proj: float32 [1024, 8, 2048], P(('dp', 'seq')), may hold values from -0.0625 to 0.0625
- norm_gains: float32 [2, 2048], replicated, may hold values from 0.5 to 1.5
- prefix_lengths: int32 [8], P('dp'), may hold values from 102 to 512
- block_slots: int32 [60], replicated, may hold values from 0 to 63, as said below
- left_stats: float32 [64, 1024, 1024], P(('dp', 'seq')), as said below
- right_stats: float32 [64, 1024, 1024], P(('dp', 'seq')), as said below
- left_roots: float32 [64, 1024, 1024], P(('dp', 'seq')), as said below
- right_inverse_roots: float32 [64, 1024, 1024], P(('dp', 'seq')), as said below
Outputs:
- layer_output: bfloat16 [8, 1024, 2048], P('dp', 'seq')
- input_grad: float32 [8, 1024, 2048], P('dp', 'seq')
- attend_in_grad: float32 [1024, 2, 4096], P(('dp', 'seq'))
- attend_out_grad: float32 [1024, 2, 2048], P(('dp', 'seq'))
- gate_up_grad: float32 [1024, 2, 16384], P(('dp', 'seq'))
- down_grad: float32 [1024, 8, 2048], P(('dp', 'seq'))
- gain_grads: float32 [2, 2048], replicated
- attend_in_new: float32 [1024, 2, 4096], P(('dp', 'seq'))
- attend_out_new: float32 [1024, 2, 2048], P(('dp', 'seq'))
- gate_up_new: float32 [1024, 2, 16384], P(('dp', 'seq'))
- down_new: float32 [1024, 8, 2048], P(('dp', 'seq'))
- gains_new: float32 [2, 2048], replicated
- left_new: float32 [64, 1024, 1024], P(('dp', 'seq'))
- right_new: float32 [64, 1024, 1024], P(('dp', 'seq'))
Inputs may be any that keep to these rules, and one draw needn't show every extreme that they name: `block_slots`: the entries are distinct; slot s is held by device s // 2 in the order of dp+seq. `left_stats`: each slot's matrix is symmetric. `right_stats`: each slot's matrix is symmetric. `left_roots`: each slot's matrix is symmetric. `right_inverse_roots`: each slot's matrix is symmetric.
All inputs are finite; a program needn't handle non-finite values.
Results may differ from a plain program's by a relative error of at most 0.018.
The roundings to bfloat16 on the way count: a program that leaves them out, or rounds other values in their place, can miss the bound.
Values may be sent and summed in bfloat16 or wider, within the bound.
No kernel may reach another device: no remote copies, remote signals or barrier semaphores. Data moves between devices by JAX's collectives and lax.ppermute only.
A program may use at most 832 MiB of HBM per device.

v0:
```python
import jax
import jax.numpy as jnp
from jax import lax
from jax.sharding import PartitionSpec as P

HEADS = 8
KV_HEADS = 4
HEAD = 256
FF = 8192
B = 1024
QD = 2048
KVD = 1024
GROUP = 2


PRECISION_MAX = lax.Precision.HIGHEST
NORM_EPS = 1e-06
ROPE_BASE = 1000042.0
STAT_DECAY = 0.5
STEP_RATE = 0.5
GAIN_RATE = 0.002
STEP_EPS = 1e-06
MASKED = -1e30


def to_blocks(weight):
    rows_here, width_count, columns = weight.shape
    shaped = weight.reshape(rows_here, width_count, columns // B, B).transpose(1, 2, 0, 3)
    return shaped.reshape(width_count * (columns // B), rows_here, B)


def from_blocks(blocks, target_shape):
    rows_here, width_count, columns = target_shape
    shaped = blocks.reshape(width_count, columns // B, rows_here, B).transpose(2, 0, 1, 3)
    return shaped.reshape(target_shape)


def rope_tables(positions):
    half_width = HEAD // 2
    frequency = ROPE_BASE ** (-2.0 * jnp.arange(half_width, dtype=jnp.float32) / HEAD)
    angles = positions[:, None] * frequency[None, :]
    return (jnp.cos(angles), jnp.sin(angles))


def rotate(tensor, cosine_table, sine_table):
    half_width = tensor.shape[-1] // 2
    front_half = tensor[..., :half_width]
    back_half = tensor[..., half_width:]
    cosine_part = cosine_table[:, None, :]
    sine_part = sine_table[:, None, :]
    return jnp.concatenate(
        [
            front_half * cosine_part - back_half * sine_part,
            back_half * cosine_part + front_half * sine_part,
        ],
        -1,
    )


def rotate_back(tensor, cosine_table, sine_table):
    half_width = tensor.shape[-1] // 2
    front_half = tensor[..., :half_width]
    back_half = tensor[..., half_width:]
    cosine_part = cosine_table[:, None, :]
    sine_part = sine_table[:, None, :]
    return jnp.concatenate(
        [
            front_half * cosine_part + back_half * sine_part,
            back_half * cosine_part - front_half * sine_part,
        ],
        -1,
    )


def project(inputs, weight):
    shaped = inputs.reshape(inputs.shape[0], weight.shape[1], weight.shape[0])
    return jnp.einsum("tkb,bkc->tc", shaped, weight, preferred_element_type=jnp.float32)


def project_back(grads, weight):
    result = jnp.einsum("tc,bkc->tkb", grads, weight, preferred_element_type=jnp.float32)
    return result.reshape(grads.shape[0], weight.shape[0] * weight.shape[1])


def weight_term(inputs, grads):
    shaped = inputs.reshape(inputs.shape[0], inputs.shape[1] // B, B)
    return jnp.einsum("tkb,tc->bkc", shaped, grads, preferred_element_type=jnp.float32)


def rms_scale(value_vectors):
    return lax.rsqrt(jnp.mean(value_vectors * value_vectors, -1, keepdims=True) + NORM_EPS)


def norm_back(value_vectors, scaler, gain, upstream):
    weighted = upstream * gain
    inner_mean = jnp.mean(weighted * value_vectors, -1, keepdims=True)
    return (
        scaler * weighted - value_vectors * scaler**3 * inner_mean,
        jnp.sum(upstream * value_vectors * scaler, 0),
    )


def attention_scores(grouped, key_all, visible):
    scores = jnp.einsum(
        "sqrgd,snrd->srgqn", grouped, key_all, preferred_element_type=jnp.float32
    ) * HEAD ** (-0.5)
    return jnp.where(visible[:, None, None], scores, MASKED)


def on_device(
    tokens,
    cotangent,
    attend_in,
    attend_out,
    gate_up,
    down_proj,
    norm_gains,
    prefix_lengths,
    block_slots,
    left_stats,
    right_stats,
    left_roots,
    right_inverse_roots,
):
    seq_count, seq_tokens, model_width = tokens.shape
    token_count = seq_count * seq_tokens
    inputs = tokens.reshape(token_count, model_width).astype(jnp.float32)
    casted = (
        attend_in.astype(jnp.bfloat16),
        attend_out.astype(jnp.bfloat16),
        gate_up.astype(jnp.bfloat16),
        down_proj.astype(jnp.bfloat16),
    )
    gathered = (
        lax.all_gather(casted[0], ("dp", "seq"), axis=0, tiled=True),
        lax.all_gather(casted[1], ("dp", "seq"), axis=0, tiled=True),
        lax.all_gather(casted[2], ("dp", "seq"), axis=0, tiled=True),
        lax.all_gather(casted[3], ("dp", "seq"), axis=0, tiled=True),
    )
    full_qkv, full_out, full_gate, full_down = gathered
    seq_rank = lax.axis_index("seq")
    query_pos = seq_rank * seq_tokens + jnp.arange(seq_tokens, dtype=jnp.int32)
    cosine_table, sine_table = rope_tables(query_pos.astype(jnp.float32))
    scale_one = rms_scale(inputs)
    normed_one = (inputs * scale_one * norm_gains[0]).astype(jnp.bfloat16)
    mixed_rows = project(normed_one, full_qkv)
    query_pre = mixed_rows[:, :QD].reshape(seq_count, seq_tokens, HEADS, HEAD)
    key_pre = mixed_rows[:, QD : QD + KVD].reshape(seq_count, seq_tokens, KV_HEADS, HEAD)
    value_rows = (
        mixed_rows[:, QD + KVD :]
        .reshape(seq_count, seq_tokens, KV_HEADS, HEAD)
        .astype(jnp.bfloat16)
    )
    query_rows = rotate(query_pre, cosine_table, sine_table).astype(jnp.bfloat16)
    key_rows = rotate(key_pre, cosine_table, sine_table).astype(jnp.bfloat16)
    key_all, value_every_head = (
        lax.all_gather(key_rows, "seq", axis=1, tiled=True),
        lax.all_gather(value_rows, "seq", axis=1, tiled=True),
    )
    key_pos = jnp.arange(key_all.shape[1], dtype=jnp.int32)
    visible = (key_pos[None, None, :] <= query_pos[None, :, None]) | (
        key_pos[None, None, :] < prefix_lengths[:, None, None]
    )
    grouped = query_rows.reshape(seq_count, seq_tokens, KV_HEADS, GROUP, HEAD)
    scores = attention_scores(grouped, key_all, visible)
    top_score = jnp.max(scores, -1, keepdims=True)
    shifted_values = jnp.exp(scores - top_score)
    total_mass = jnp.sum(shifted_values, -1, keepdims=True)
    log_total = top_score + jnp.log(total_mass)
    shares_low = (shifted_values / total_mass).astype(jnp.bfloat16)
    attended = jnp.einsum(
        "srgqn,snrd->sqrgd", shares_low, value_every_head, preferred_element_type=jnp.float32
    )
    attended_low = attended.reshape(token_count, QD).astype(jnp.bfloat16)
    middle = inputs + project(attended_low, full_out)
    scale_two = rms_scale(middle)
    normed_two = (middle * scale_two * norm_gains[1]).astype(jnp.bfloat16)
    gate_rows = project(normed_two, full_gate)
    gate_part = gate_rows[:, :FF]
    up_part = gate_rows[:, FF:]
    sigmoid_gate = jax.nn.sigmoid(gate_part)
    hidden = (gate_part * sigmoid_gate * up_part).astype(jnp.bfloat16)
    result = middle + project(hidden, full_down)
    layer_output = result.astype(jnp.bfloat16).reshape(tokens.shape)
    again = (
        lax.all_gather(casted[0], ("dp", "seq"), axis=0, tiled=True),
        lax.all_gather(casted[1], ("dp", "seq"), axis=0, tiled=True),
        lax.all_gather(casted[2], ("dp", "seq"), axis=0, tiled=True),
        lax.all_gather(casted[3], ("dp", "seq"), axis=0, tiled=True),
    )
    back_qkv, back_out, back_gate, back_down = again
    upstream = cotangent.reshape(token_count, model_width)
    hidden_grad = project_back(upstream, back_down)
    gate_grad = hidden_grad * up_part * sigmoid_gate * (1.0 + gate_part * (1.0 - sigmoid_gate))
    up_grad = hidden_grad * gate_part * sigmoid_gate
    gate_up_rows = jnp.concatenate([gate_grad, up_grad], 1).astype(jnp.bfloat16)
    normed_two_grad = project_back(gate_up_rows, back_gate)
    middle_grad, gain_two = norm_back(middle, scale_two, norm_gains[1], normed_two_grad)
    middle_grad = middle_grad + upstream.astype(jnp.float32)
    branch_grad = middle_grad.astype(jnp.bfloat16)
    attended_grad = project_back(branch_grad, back_out).astype(jnp.bfloat16)
    scores_again = attention_scores(grouped, key_all, visible)
    shares_again = jnp.exp(scores_again - log_total)
    grad_heads = attended_grad.reshape(seq_count, seq_tokens, KV_HEADS, GROUP, HEAD)
    share_grad = jnp.einsum(
        "sqrgd,snrd->srgqn", grad_heads, value_every_head, preferred_element_type=jnp.float32
    )
    inner_sum = jnp.sum(shares_again * share_grad, -1, keepdims=True)
    score_grad = (shares_again * (share_grad - inner_sum)).astype(jnp.bfloat16)
    query_grad = jnp.einsum(
        "srgqn,snrd->sqrgd", score_grad, key_all, preferred_element_type=jnp.float32
    ) * HEAD ** (-0.5)
    key_grad_all = jnp.einsum(
        "srgqn,sqrgd->snrd", score_grad, grouped, preferred_element_type=jnp.float32
    ) * HEAD ** (-0.5)
    value_grad_all = jnp.einsum(
        "srgqn,sqrgd->snrd",
        shares_again.astype(jnp.bfloat16),
        grad_heads,
        preferred_element_type=jnp.float32,
    )
    key_grad, value_grad = (
        lax.psum_scatter(
            key_grad_all.astype(jnp.bfloat16), "seq", scatter_dimension=1, tiled=True
        ).astype(jnp.float32),
        lax.psum_scatter(
            value_grad_all.astype(jnp.bfloat16), "seq", scatter_dimension=1, tiled=True
        ).astype(jnp.float32),
    )
    query_grad = rotate_back(
        query_grad.reshape(seq_count, seq_tokens, HEADS, HEAD), cosine_table, sine_table
    )
    key_grad = rotate_back(key_grad, cosine_table, sine_table)
    mixed_grad = jnp.concatenate(
        [
            query_grad.reshape(token_count, QD),
            key_grad.reshape(token_count, KVD),
            value_grad.reshape(token_count, KVD),
        ],
        1,
    ).astype(jnp.bfloat16)
    normed_one_grad = project_back(mixed_grad, back_qkv)
    input_grad, gain_one = norm_back(inputs, scale_one, norm_gains[0], normed_one_grad)
    input_grad = (input_grad + middle_grad).reshape(tokens.shape)
    gain_first, gain_second = lax.psum((gain_one, gain_two), ("dp", "seq"))
    gain_grads = jnp.stack([gain_first, gain_second], 0)
    qkv_summed = lax.psum_scatter(
        weight_term(normed_one, mixed_grad), ("dp", "seq"), scatter_dimension=0, tiled=True
    )
    out_summed = lax.psum_scatter(
        weight_term(attended_low, branch_grad), ("dp", "seq"), scatter_dimension=0, tiled=True
    )
    gate_summed = lax.psum_scatter(
        weight_term(normed_two, gate_up_rows), ("dp", "seq"), scatter_dimension=0, tiled=True
    )
    down_summed = lax.psum_scatter(
        weight_term(hidden, upstream), ("dp", "seq"), scatter_dimension=0, tiled=True
    )
    grad_list = [qkv_summed, out_summed, gate_summed, down_summed]
    weight_list = (attend_in, attend_out, gate_up, down_proj)
    devices = lax.axis_size(("dp", "seq"))
    slots_here = left_stats.shape[0]
    total_slots = slots_here * devices
    owner_table = (
        block_slots[None, :] == jnp.arange(total_slots, dtype=jnp.int32)[:, None]
    ).astype(jnp.float32)
    grad_blocks = jnp.concatenate([to_blocks(grad) for grad in grad_list], 0)
    weight_blocks = jnp.concatenate([to_blocks(weight) for weight in weight_list], 0)
    send_grad = jnp.einsum("sb,bxy->sxy", owner_table, grad_blocks, precision=PRECISION_MAX)
    send_weight = jnp.einsum("sb,bxy->sxy", owner_table, weight_blocks, precision=PRECISION_MAX)
    owned_grad, owned_weight = (
        lax.all_to_all(
            send_grad.astype(jnp.bfloat16), ("dp", "seq"), split_axis=0, concat_axis=1, tiled=True
        ).astype(send_grad.dtype),
        lax.all_to_all(
            send_weight.astype(jnp.bfloat16), ("dp", "seq"), split_axis=0, concat_axis=1, tiled=True
        ).astype(send_weight.dtype),
    )
    left_new = STAT_DECAY * left_stats + (1.0 - STAT_DECAY) * jnp.einsum(
        "sij,skj->sik", owned_grad, owned_grad, precision=PRECISION_MAX
    )
    right_new = STAT_DECAY * right_stats + (1.0 - STAT_DECAY) * jnp.einsum(
        "sji,sjk->sik", owned_grad, owned_grad, precision=PRECISION_MAX
    )
    left_applied = jnp.einsum("sij,sjk->sik", left_roots, owned_grad, precision=PRECISION_MAX)
    direction = jnp.einsum(
        "sij,sjk->sik", left_applied, right_inverse_roots, precision=PRECISION_MAX
    )
    weight_size = jnp.sqrt(jnp.mean(owned_weight * owned_weight, (1, 2), keepdims=True) + STEP_EPS)
    direction_size = jnp.sqrt(jnp.mean(direction * direction, (1, 2), keepdims=True) + STEP_EPS)
    updated = owned_weight - STEP_RATE * weight_size / direction_size * direction
    returned = lax.all_to_all(
        updated.astype(jnp.bfloat16), ("dp", "seq"), split_axis=1, concat_axis=0, tiled=True
    ).astype(updated.dtype)
    new_blocks = jnp.einsum("sb,sxy->bxy", owner_table, returned, precision=PRECISION_MAX)
    new_weights = []
    offset = 0
    for weight in weight_list:
        block_count = weight.shape[1] * (weight.shape[2] // B)
        new_weights.append(from_blocks(new_blocks[offset : offset + block_count], weight.shape))
        offset = offset + block_count
    gains_new = norm_gains - GAIN_RATE * gain_grads
    return (
        layer_output,
        input_grad,
        grad_list[0],
        grad_list[1],
        grad_list[2],
        grad_list[3],
        gain_grads,
        new_weights[0],
        new_weights[1],
        new_weights[2],
        new_weights[3],
        gains_new,
        left_new,
        right_new,
    )


def solution(mesh):
    return jax.shard_map(
        on_device,
        mesh=mesh,
        in_specs=(
            P("dp", "seq", None),
            P("dp", "seq", None),
            P(("dp", "seq"), None, None),
            P(("dp", "seq"), None, None),
            P(("dp", "seq"), None, None),
            P(("dp", "seq"), None, None),
            P(),
            P("dp"),
            P(),
            P(("dp", "seq"), None, None),
            P(("dp", "seq"), None, None),
            P(("dp", "seq"), None, None),
            P(("dp", "seq"), None, None),
        ),
        out_specs=(
            P("dp", "seq", None),
            P("dp", "seq", None),
            P(("dp", "seq"), None, None),
            P(("dp", "seq"), None, None),
            P(("dp", "seq"), None, None),
            P(("dp", "seq"), None, None),
            P(),
            P(("dp", "seq"), None, None),
            P(("dp", "seq"), None, None),
            P(("dp", "seq"), None, None),
            P(("dp", "seq"), None, None),
            P(),
            P(("dp", "seq"), None, None),
            P(("dp", "seq"), None, None),
        ),
        check_vma=False,
    )
```

profile of v0, /device:TPU:0, one launch (start us, length us, event | category | flops | bytes accessed | tf_op | source)
XLA Modules:
  0.0 5604.1 jit_solution(3400685009401329004)
XLA Ops:
  15.2 113.9 %all-gather.7.cloned.1.call-done = bf16[1024,2,4096]{2,0,1:T(8,128)(2,1)} async-done(((bf16[32,2,4096]{2,0,1:T(8,128)(2,1)}), bf16[1024,2,4096]{2,0,1:T(8,128)(2,1)}) %all-gather.7.cloned.1.call-update) | async-done | bytes 16777232 | tf_op jit(solution)/shard_map/all_gather | solution.py:135
  163.9 26.5 all-gather.11.cloned.1.call-done
  197.8 39.7 all-gather.9.cloned.1.call-done
  244.2 72.5 %all-gather.13.cloned.1.call-done = bf16[1024,2,2048]{2,0,1:T(8,128)(2,1)} async-done(((bf16[32,2,2048]{2,0,1:T(8,128)(2,1)}), bf16[1024,2,2048]{2,0,1:T(8,128)(2,1)}) %all-gather.13.cloned.1.call-update) | async-done | bytes 8388624 | tf_op jit(solution)/shard_map/all_gather | solution.py:136
  323.1 190.4 %all-gather.17.cloned.1.call-done = bf16[1024,8,2048]{2,0,1:T(8,128)(2,1)} async-done(((bf16[32,8,2048]{2,0,1:T(8,128)(2,1)}), bf16[1024,8,2048]{2,0,1:T(8,128)(2,1)}) %all-gather.17.cloned.1.call-update) | async-done | bytes 33554448 | tf_op jit(solution)/shard_map/all_gather | solution.py:138
  513.5 19.9 fusion.76
  542.4 329.0 %all-gather.15.cloned.1.call-done = bf16[1024,2,16384]{2,0,1:T(8,128)(2,1)} async-done(((bf16[32,2,16384]{2,0,1:T(8,128)(2,1)}), bf16[1024,2,16384]{2,0,1:T(8,128)(2,1)}) %all-gather.15.cloned.1.call-update) | async-done | bytes 67108880 | tf_op jit(solution)/shard_map/all_gather | solution.py:137
  871.4 32.1 convolution_bitcast_fusion.2
  918.6 28.7 fusion.63
  984.7 25.5 copy.280
  1019.7 29.7 reduce-scatter.4.cloned.1.call-done
  1055.6 16.0 convolution_bitcast_fusion.3
  1071.6 50.1 copy.277
  1122.9 49.2 convolution_bitcast_fusion
  1172.2 194.7 %copy.283 = f32[1024,2,16384]{2,1,0:T(2,128)} copy(f32[1024,2,16384]{0,2,1:T(8,128)} %convolution_bitcast_fusion) | data formatting | bytes 268435456 | tf_op jit(solution)/shard_map/tkb,tc->bkc/transpose | solution.py:87
  1373.8 28.0 convolution_bitcast_fusion.1
  1443.2 483.9 %all-reduce.8.cloned.1.call-done = f32[1024,2,4096]{2,1,0:T(2,128)} async-done(((f32[1024,2,4096]{2,1,0:T(2,128)}), f32[1024,2,4096]{2,1,0:T(2,128)}) %all-reduce.8.cloned.1.call-update) | async-done | bytes 33554448
  1929.9 1882.2 %all-reduce.12.cloned.1.call-done = f32[1024,2,16384]{2,1,0:T(2,128)} async-done(((f32[1024,2,16384]{2,1,0:T(2,128)}), f32[1024,2,16384]{2,1,0:T(2,128)}) %all-reduce.12.cloned.1.call-update) | async-done | bytes 134217744
  3823.5 1401.0 %reduce-scatter.8.cloned.1.call-done = f32[32,8,2048]{2,0,1:T(8,128)} async-done(((f32[1024,8,2048]{2,0,1:T(8,128)}), f32[32,8,2048]{2,0,1:T(8,128)}) %reduce-scatter.8.cloned.1.call-update) | async-done | bytes 2097168 | tf_op jit(solution)/shard_map/reduce_scatter | solution.py:256
  5262.1 81.9 %all-to-all-done.1 = bf16[64,32,1024]{2,1,0:T(8,128)(2,1)} async-done(((bf16[64,32,1024]{2,1,0:T(8,128)(2,1)}), bf16[64,32,1024]{2,1,0:T(8,128)(2,1)}, u32[]{:S(2)}, u32[]{:S(2)}) %all-to-all-start.1) | async-done | bytes 4194336 | tf_op jit(solution)/shard_map/all_to_all | solution.py:272
  5347.1 17.4 fusion.104
  5364.6 29.6 multiply_reduce_fusion
  5415.0 17.1 fusion.40
  5448.7 81.0 %all-reduce.3 = (f32[1,2048]{1,0:T(1,128)S(1)}, f32[1,2048]{1,0:T(1,128)S(1)}) all-reduce(f32[1,2048]{1,0:T(1,128)S(1)} %bitcast.360, f32[1,2048]{1,0:T(1,128)S(1)} %bitcast.361), channel_id=1, replica_groups=mesh['dp'=8,'seq'=4] {'dp','seq'}, use_global_device_ids=true, to_apply=%region_16.17 | all-reduce | flops 4096 | bytes 32768 | tf_op jit(solution)/shard_map/psum | solution.py:245
  (264 shorter events, 348.0 us)
Async XLA Ops:
  7.2 121.9 %all-gather.7.cloned.1.call-start = ((), (), s32[]{:S(2)}) async-start(), calls=%async_computation.6 | async-start | bytes 17301504 | tf_op jit(solution)/shard_map/all_gather | solution.py:135
  9.9 180.4 %all-gather.11.cloned.1.call-start = ((), (), s32[]{:S(2)}) async-start(), calls=%async_computation.8 | async-start | bytes 2621440 | tf_op jit(solution)/shard_map/all_gather | solution.py:157
  13.2 124.7 %copy-start.13 = (f32[256,2,1024]{2,1,0:T(2,128)}, f32[256,2,1024]{2,1,0:T(2,128)S(1)}, u32[]{:S(2)}) copy-start(f32[256,2,1024]{2,1,0:T(2,128)S(1)} %reshape.564) | copy-start | bytes 6291460
  13.8 124.0 %copy-start.39 = (f32[2,1024]{1,0:T(2,128)}, f32[2,1024]{1,0:T(2,128)S(1)}, u32[]{:S(2)}) copy-start(f32[2,1024]{1,0:T(2,128)S(1)} %mul.368) | copy-start | bytes 24580
  14.7 123.2 %copy-start.46 = (f32[256]{0:T(256)}, f32[256]{0:T(256)S(1)}, u32[]{:S(2)}) copy-start(f32[256]{0:T(256)S(1)} %get-tuple-element.113) | copy-start | bytes 3076
  15.2 148.1 %copy-start.27 = (f32[256,128]{1,0:T(8,128)}, f32[256,128]{1,0:T(8,128)S(1)}, u32[]{:S(2)}) copy-start(f32[256,128]{1,0:T(8,128)S(1)} %get-tuple-element.110) | copy-start | bytes 393220
  15.2 148.1 %copy-start.29 = (f32[256,128]{1,0:T(8,128)}, f32[256,128]{1,0:T(8,128)S(1)}, u32[]{:S(2)}) copy-start(f32[256,128]{1,0:T(8,128)S(1)} %get-tuple-element.111) | copy-start | bytes 393220
  146.1 91.4 %all-gather.9.cloned.1.call-start = ((), (), s32[]{:S(2)}) async-start(), calls=%async_computation.7 | async-start | bytes 2621440 | tf_op jit(solution)/shard_map/all_gather | solution.py:158
  150.3 166.4 %all-gather.13.cloned.1.call-start = ((), (), s32[]{:S(2)}) async-start(), calls=%async_computation.9 | async-start | bytes 8650752 | tf_op jit(solution)/shard_map/all_gather | solution.py:136
  152.4 361.1 %all-gather.17.cloned.1.call-start = ((), (), s32[]{:S(2)}) async-start(), calls=%async_computation.11 | async-start | bytes 34603008 | tf_op jit(solution)/shard_map/all_gather | solution.py:138
  154.6 716.8 %all-gather.15.cloned.1.call-start = ((), (), s32[]{:S(2)}) async-start(), calls=%async_computation.10 | async-start | bytes 69206016 | tf_op jit(solution)/shard_map/all_gather | solution.py:137
  160.5 856.8 %reduce-scatter.6.cloned.1.call-start = ((), (), s32[]{:S(2)}) async-start(), calls=%async_computation.13 | async-start | bytes 2621440 | tf_op jit(solution)/shard_map/reduce_scatter | solution.py:226
  322.8 627.7 %copy-start.1 = (f32[256,2048]{1,0:T(8,128)}, f32[256,2048]{1,0:T(8,128)S(1)}, u32[]{:S(2)}) copy-start(f32[256,2048]{1,0:T(8,128)S(1)} %get-tuple-element.119) | copy-start | bytes 6291460
  323.1 548.2 %copy-start.18 = (bf16[256,2048]{1,0:T(8,128)(2,1)}, bf16[256,2048]{1,0:T(8,128)(2,1)S(1)}, u32[]{:S(2)}) copy-start(bf16[256,2048]{1,0:T(8,128)(2,1)S(1)} %multiply_convert_fusion.3) | copy-start | bytes 3145732
  961.6 87.8 %reduce-scatter.4.cloned.1.call-start = ((), (), s32[]{:S(2)}) async-start(), calls=%async_computation.12 | async-start | bytes 2621440 | tf_op jit(solution)/shard_map/reduce_scatter | solution.py:223
  976.2 464.0 %all-reduce.10.cloned.1.call-start = ((), (), s32[]{:S(2)}) async-start(), calls=%async_computation.16 | async-start | bytes 33554432
  1010.2 916.9 %all-reduce.8.cloned.1.call-start = ((), (), s32[]{:S(2)}) async-start(), calls=%async_computation.15 | async-start | bytes 67108864
  1121.7 2690.4 %all-reduce.12.cloned.1.call-start = ((), (), s32[]{:S(2)}) async-start(), calls=%async_computation.17 | async-start | bytes 268435456
  1366.8 3857.6 %reduce-scatter.8.cloned.1.call-start = ((), (), s32[]{:S(2)}) async-start(), calls=%async_computation.14 | async-start | bytes 69206016 | tf_op jit(solution)/shard_map/reduce_scatter | solution.py:256
  1435.5 3811.1 %all-to-all-start = ((bf16[64,32,1024]{2,1,0:T(8,128)(2,1)}), bf16[64,32,1024]{2,1,0:T(8,128)(2,1)}, u32[]{:S(2)}, u32[]{:S(2)}) async-start(bf16[64,32,1024]{2,1,0:T(8,128)(2,1)} %copy.288), calls=%async_computation.3 | async-start | bytes 8388608 | tf_op jit(solution)/shard_map/all_to_all | solution.py:275
  1928.4 1888.4 %copy-start.20 = (f32[32,2,4096]{2,1,0:T(2,128)}, f32[32,2,4096]{2,1,0:T(2,128)S(1)}, u32[]{:S(2)}) copy-start(f32[32,2,4096]{2,1,0:T(2,128)S(1)} %constant_dynamic-slice_fusion.2) | copy-start | bytes 3145732
  5246.6 97.4 %all-to-all-start.1 = ((bf16[64,32,1024]{2,1,0:T(8,128)(2,1)}), bf16[64,32,1024]{2,1,0:T(8,128)(2,1)}, u32[]{:S(2)}, u32[]{:S(2)}) async-start(bf16[64,32,1024]{2,1,0:T(8,128)(2,1)} %copy.292), calls=%async_computation.4 | async-start | bytes 8388608 | tf_op jit(solution)/shard_map/all_to_all | solution.py:272
  5408.9 144.1 %all-to-all-start.2 = ((bf16[2,1024,1024]{2,0,1:T(2,128)(2,1)}), bf16[2,1024,1024]{2,0,1:T(2,128)(2,1)}, u32[]{:S(2)}, u32[]{:S(2)}) async-start(bf16[2,1024,1024]{2,0,1:T(2,128)(2,1)} %copy.296), calls=%async_computation.5 | async-start | bytes 8388608 | tf_op jit(solution)/shard_map/all_to_all | solution.py:292
  5445.3 85.0 %copy-start.5 = (f32[256,2048]{1,0:T(8,128)S(1)}, f32[256,2048]{1,0:T(8,128)}, u32[]{:S(2)}) copy-start(f32[256,2048]{1,0:T(8,128)} %copy-done.3) | copy-start | bytes 6291460
  (49 other events, 864.2 us)
Sparse Core Ops, SparseCore 0:
  11.6 117.4 all-gather.6
  146.2 44.0 all-gather.10
  192.5 44.9 all-gather.8
  241.0 75.6 all-gather.12
  320.2 193.3 all-gather.16
  517.0 354.3 all-gather.14
  961.7 42.0 reduce-scatter.5
  1006.2 43.1 reduce-scatter.3
  1055.4 277.3 all-reduce.9
  1339.0 588.0 all-reduce.7
  1934.7 1877.3 all-reduce.11
  3814.4 1409.9 reduce-scatter.7
where the time goes:
time: 5620 us; the launch traced here: 5600 us
  waiting for transfers between devices  4650 us (83%)
  local copies, waits for them, and re-layouts  453 us (8%)
  matrix products  341 us (6%)
  blocking collectives  81 us (1%)
    unnamed x15, waiting for transfers between devices  2370 us
    reduce_scatter x1, waiting for transfers between devices, on_device(): lax.psum_scatter(weight_term(hidden, upstream), ('dp', 'seq'), scatter_di...  1400 us
    all_gather x1, waiting for transfers between devices, on_device(): lax.all_gather(casted[2], ('dp', 'seq'), axis=0, tiled=True)  329 us
    transpose x3, local copies, waits for them, and re-layouts, weight_term(): jnp.einsum('tkb,tc->bkc', shaped, grads, preferred_element_type=jnp.float32)  270 us
    all_gather x1, waiting for transfers between devices, on_device(): lax.all_gather(casted[3], ('dp', 'seq'), axis=0, tiled=True)  190 us
    all_gather x1, waiting for transfers between devices, on_device(): lax.all_gather(casted[0], ('dp', 'seq'), axis=0, tiled=True)  114 us
  transfers between devices with their start and end apart: 15, of which 11 were waited for; matrix products, arithmetic and copies ran while one was open for 11% of the time, Pallas kernels for 0%

commit v1 on v0

v1 whole, which is shorter than its diff:
```python
import jax
import jax.numpy as jnp
from jax import lax
from jax.sharding import Mesh
from jax.sharding import PartitionSpec as P

D = 2048
HEADS = 8
KV_HEADS = 4
HEAD = 256
FF = 8192
B = 1024
QD = 2048
KVD = 1024
TP = 8

NORM_EPS = 1e-06
ROPE_BASE = 1000042.0
STAT_DECAY = 0.5
STEP_RATE = 0.5
GAIN_RATE = 0.002
STEP_EPS = 1e-06
MASKED = -1e30

BF = jnp.bfloat16
F32 = jnp.float32
TENSOR = ("a", "b", "c")
SHARD = ("o", "z")
ALL = ("o", "a", "b", "c", "z")


def dot(x, y, out=F32):
    return lax.dot_general(x, y, (((1,), (0,)), ((), ())), preferred_element_type=F32).astype(out)


def dot_nt(x, y, out=F32):
    return lax.dot_general(x, y, (((1,), (1,)), ((), ())), preferred_element_type=F32).astype(out)


def dot_tn(x, y, out=F32):
    return lax.dot_general(x, y, (((0,), (0,)), ((), ())), preferred_element_type=F32).astype(out)


def flip(value, axis):
    return lax.ppermute(value, axis, [(0, 1), (1, 0)])


def gather_tokens(value):
    half = value.shape[0] // 2
    p, q = value[:half], value[half:]
    p_b = flip(p, "b")
    q_a = flip(q, "a")
    p_near = jnp.concatenate([p, p_b], 0)
    q_near = jnp.concatenate([q, q_a], 0)
    p_far = flip(p_near, "a")
    q_far = flip(q_near, "b")
    mine = jnp.concatenate([p_near, p_far, q_near, q_far], 0)
    return jnp.concatenate([mine, flip(mine, "c")], 0)


def relative_order(piece):
    parts = {xor: piece(xor) for xor in range(TP)}
    half = parts[0].shape[0] // 2
    order = []
    for c in (0, 1):
        order += [parts[x + c][:half] for x in (0, 2, 4, 6)]
        order += [parts[x + c][half:] for x in (0, 4, 2, 6)]
    return jnp.concatenate(order, 0)


def scatter_tokens(partial):
    half = partial.shape[0] // 2
    near = partial[:half].astype(F32) + flip(partial[half:], "c").astype(F32)
    quarter = half // 2
    p, q = near[:quarter], near[quarter:]
    e = quarter // 2
    p_sum = p[:e] + flip(p[e:].astype(BF), "a").astype(F32)
    q_sum = q[:e] + flip(q[e:].astype(BF), "b").astype(F32)
    f = e // 2
    p_out = p_sum[:f] + flip(p_sum[f:].astype(BF), "b").astype(F32)
    q_out = q_sum[:f] + flip(q_sum[f:].astype(BF), "a").astype(F32)
    return jnp.concatenate([p_out, q_out], 0)


def swap_halves(value):
    half = value.shape[0] // 2
    return jnp.concatenate([value[half:], value[:half]], 0)


def exchange(value, axes):
    return lax.all_to_all(value, axes, split_axis=0, concat_axis=0, tiled=True)


def reshard(tokens, z_count):
    seqs, length, width = tokens.shape
    n = length // TP
    parts = exchange(tokens.reshape(seqs, TP, n, width).transpose(1, 0, 2, 3), TENSOR)
    m = TP * seqs // z_count
    parts = exchange(parts.reshape(z_count, m, n, width), "z")
    return parts.transpose(1, 0, 2, 3).reshape(m, z_count * n, width)


def reshard_back(values, z_count, seqs):
    m, rows, width = values.shape
    n = rows // z_count
    parts = exchange(values.reshape(m, z_count, n, width).transpose(1, 0, 2, 3), "z")
    parts = exchange(parts.reshape(TP, seqs, n, width), TENSOR)
    return parts.transpose(1, 0, 2, 3).reshape(seqs, TP * n, width)


def rms_scale(value):
    return lax.rsqrt(jnp.mean(value * value, -1, keepdims=True) + NORM_EPS)


def norm_back(value, scaler, gain, upstream):
    weighted = upstream * gain
    inner_mean = jnp.mean(weighted * value, -1, keepdims=True)
    return (
        scaler * weighted - value * scaler**3 * inner_mean,
        jnp.sum(upstream * value * scaler, 0),
    )


def rotate(value, cosine, sine):
    front, back = value[:, : HEAD // 2], value[:, HEAD // 2 :]
    return jnp.concatenate([front * cosine - back * sine, back * cosine + front * sine], 1)


def attend(query, key, value, visible):
    scores = jnp.where(visible, dot_nt(query, key) * HEAD ** (-0.5), MASKED)
    top = jnp.max(scores, -1, keepdims=True)
    shifted = jnp.exp(scores - top)
    mass = jnp.sum(shifted, -1, keepdims=True)
    out = dot((shifted / mass).astype(BF), value, BF)
    return out, top + jnp.log(mass)


def attend_back(query, key, value, visible, log_total, out_grad):
    scores = jnp.where(visible, dot_nt(query, key) * HEAD ** (-0.5), MASKED)
    shares = jnp.exp(scores - log_total)
    share_grad = dot_nt(out_grad, value)
    inner = jnp.sum(shares * share_grad, -1, keepdims=True)
    score_grad = (shares * (share_grad - inner)).astype(BF)
    query_grad = dot(score_grad, key) * HEAD ** (-0.5)
    key_grad = dot_tn(score_grad, query) * HEAD ** (-0.5)
    value_grad = dot_tn(shares.astype(BF), out_grad)
    return query_grad, key_grad, value_grad


def on_device(
    tokens,
    cotangent,
    attend_in,
    attend_out,
    gate_up,
    down_proj,
    norm_gains,
    prefix_lengths,
    block_slots,
    left_stats,
    right_stats,
    left_roots,
    right_inverse_roots,
):
    outer, z_count = lax.axis_size("o"), lax.axis_size("z")
    shards = outer * z_count
    devices = shards * TP
    rank = lax.axis_index(TENSOR)
    core = lax.axis_index("c")
    z_rank = lax.axis_index("z")
    seqs, z_tokens, width = tokens.shape
    n = z_tokens // TP
    m = TP * seqs // z_count
    rows = attend_in.shape[0]

    x = reshard(tokens, z_count).astype(F32)
    x = [x[i] for i in range(m)]

    def to_full(parts, lead):
        columns = parts.shape[-1]
        every = lax.all_gather(parts, SHARD, axis=0, tiled=False)
        every = every.reshape(outer, z_count, TP, lead, rows, columns)
        return every.transpose(3, 0, 2, 1, 4, 5).reshape(lead * B, columns)

    low_in = attend_in.astype(BF)
    heads = low_in[:, :, :QD].reshape(rows, 2, HEADS, HEAD)
    keys_values = low_in[:, :, QD:].reshape(rows, 2, 2, KV_HEADS, HEAD).transpose(0, 1, 3, 2, 4)
    mixed_cols = jnp.concatenate([heads, keys_values.reshape(rows, 2, HEADS, HEAD)], -1)
    w_mix = to_full(exchange(mixed_cols.transpose(2, 1, 0, 3), TENSOR), 2)

    low_out = attend_out.astype(BF).transpose(1, 0, 2)
    holders = range(outer * TP)
    span = 2 * outer

    def home(g, k):
        return (g % span) // 2 * TP + g // span + 4 * k

    to_same = [(g, home(g, g % 2)) for g in holders]
    to_other = [(g, home(g, 1 - g % 2)) for g in holders]
    dp_axes = ("o",) + TENSOR
    odd = lax.axis_index(dp_axes) % 2
    upper = rank // 4
    same = jnp.where(odd == 0, low_out[0], low_out[1])
    other = jnp.where(odd == 0, low_out[1], low_out[0])
    same = lax.ppermute(same, dp_axes, to_same)
    other = lax.ppermute(other, dp_axes, to_other)
    pair = jnp.where(upper == 0, jnp.stack([same, other]), jnp.stack([other, same]))
    w_out = lax.all_gather(pair, SHARD, axis=0, tiled=False)
    w_out = w_out.reshape(outer, z_count, 2, rows, D).transpose(0, 2, 1, 3, 4).reshape(HEAD, D)

    cut_gate = gate_up.astype(BF).reshape(rows, 2, 2, TP, FF // TP).transpose(3, 1, 0, 2, 4)
    w_gate = to_full(exchange(cut_gate.reshape(TP, 2, rows, 2 * FF // TP), TENSOR), 2)
    w_down = to_full(exchange(down_proj.astype(BF).transpose(1, 0, 2), TENSOR), 1)

    def positions_of(xor):
        base = (rank ^ xor) * n
        return (
            jnp.arange(z_count, dtype=jnp.int32)[:, None] * z_tokens
            + base
            + jnp.arange(n, dtype=jnp.int32)[None, :]
        ).reshape(-1)

    positions = relative_order(positions_of)
    frequency = ROPE_BASE ** (-2.0 * jnp.arange(HEAD // 2, dtype=F32) / HEAD)
    angles = positions.astype(F32)[:, None] * frequency[None, :]
    cosine, sine = jnp.cos(angles), jnp.sin(angles)
    prefixes = exchange(jnp.broadcast_to(prefix_lengths[None], (TP, seqs)), TENSOR).reshape(-1)
    prefixes = lax.dynamic_slice_in_dim(prefixes, z_rank * m, m)
    visible = [
        (positions[None, :] <= positions[:, None]) | (positions[None, :] < prefixes[i])
        for i in range(m)
    ]

    scale_one, normed_one, query, key, value, attended, log_total = [], [], [], [], [], [], []
    middle, scale_two, normed_two = [], [], []
    for i in range(m):
        scale_one.append(rms_scale(x[i]))
        normed_one.append(gather_tokens((x[i] * scale_one[i] * norm_gains[0]).astype(BF)))
        mixed = dot(normed_one[i], w_mix)
        query.append(rotate(mixed[:, :HEAD], cosine, sine).astype(BF))
        own = mixed[:, HEAD:]
        own = jnp.where(core == 0, rotate(own, cosine, sine), own).astype(BF)
        got = swap_halves(flip(own, "c"))
        key.append(jnp.where(core == 0, own, got))
        value.append(jnp.where(core == 0, got, own))
        out, total = attend(query[i], key[i], value[i], visible[i])
        attended.append(out)
        log_total.append(total)
    for i in range(m):
        middle.append(x[i] + scatter_tokens(dot(attended[i], w_out, BF)))
        scale_two.append(rms_scale(middle[i]))
        normed_two.append(gather_tokens((middle[i] * scale_two[i] * norm_gains[1]).astype(BF)))
    down_in = reshard(cotangent, z_count)
    upstream = [gather_tokens(down_in[i]) for i in range(m)]
    hidden, gate_rows, layer_out = [], [], []
    for i in range(m):
        both = dot(normed_two[i], w_gate)
        gate, up = both[:, : FF // TP], both[:, FF // TP :]
        sigmoid = jax.nn.sigmoid(gate)
        hidden.append((gate * sigmoid * up).astype(BF))
        hidden_grad = dot_nt(upstream[i], w_down)
        gate_grad = hidden_grad * up * sigmoid * (1.0 + gate * (1.0 - sigmoid))
        up_grad = hidden_grad * gate * sigmoid
        gate_rows.append(jnp.concatenate([gate_grad, up_grad], 1).astype(BF))
        layer_out.append(middle[i] + scatter_tokens(dot(hidden[i], w_down, BF)))

    join = lambda parts: jnp.concatenate(parts, 0)

    def to_owners(grad, lead):
        columns = grad.shape[-1]
        grad = grad.reshape(lead, outer, TP, z_count, rows, columns).transpose(1, 3, 2, 0, 4, 5)
        grad = grad.reshape(shards * TP * lead * rows, columns)
        grad = lax.psum_scatter(grad, SHARD, scatter_dimension=0, tiled=True)
        return grad.reshape(TP, lead, rows, columns)

    g_down = exchange(to_owners(dot_tn(join(hidden), join(upstream), BF), 1), TENSOR)
    g_gate = exchange(to_owners(dot_tn(join(normed_two), join(gate_rows), BF), 2), TENSOR)
    middle_grad, branch, gain_two = [], [], 0.0
    for i in range(m):
        normed_grad = scatter_tokens(dot_nt(gate_rows[i], w_gate, BF))
        grad, gain = norm_back(middle[i], scale_two[i], norm_gains[1], normed_grad)
        gain_two = gain_two + gain
        middle_grad.append(grad + down_in[i].astype(F32))
        branch.append(gather_tokens(middle_grad[i].astype(BF)))
    g_out = dot_tn(join(attended), join(branch), BF)
    g_out = g_out.reshape(outer, 2, z_count, rows, D).transpose(0, 2, 1, 3, 4).reshape(shards, 2, rows, D)
    g_out = lax.psum_scatter(g_out, SHARD, scatter_dimension=0, tiled=False)
    mixed_grad, input_grad, gain_one = [], [], 0.0
    for i in range(m):
        attended_grad = dot_nt(branch[i], w_out, BF)
        query_grad, key_grad, value_grad = attend_back(
            query[i], key[i], value[i], visible[i], log_total[i], attended_grad
        )
        keep = jnp.where(core == 0, key_grad, value_grad)
        give = jnp.where(core == 0, value_grad, key_grad)
        keep = keep + swap_halves(flip(give, "c"))
        keep = jnp.where(core == 0, rotate(keep, cosine, -sine), keep)
        mixed_grad.append(
            jnp.concatenate([rotate(query_grad, cosine, -sine), keep], 1).astype(BF)
        )
    g_mix = exchange(to_owners(dot_tn(join(normed_one), join(mixed_grad), BF), 2), TENSOR)
    for i in range(m):
        normed_grad = scatter_tokens(dot_nt(mixed_grad[i], w_mix, BF))
        grad, gain = norm_back(x[i], scale_one[i], norm_gains[0], normed_grad)
        gain_one = gain_one + gain
        input_grad.append(grad + middle_grad[i])
    layer_output = reshard_back(jnp.stack(layer_out).astype(BF), z_count, seqs)
    input_grad = reshard_back(jnp.stack(input_grad).astype(BF), z_count, seqs).astype(F32)

    g_heads = g_mix[..., :HEAD].transpose(2, 1, 0, 3).reshape(rows, 2, QD)
    g_kv = g_mix[..., HEAD:].reshape(KV_HEADS, 2, 2, rows, HEAD).transpose(3, 2, 1, 0, 4)
    grad_in = jnp.concatenate([g_heads, g_kv.reshape(rows, 2, 2 * KVD)], -1)
    first = jnp.where(upper == 0, g_out[0], g_out[1])
    second = jnp.where(upper == 0, g_out[1], g_out[0])
    first = lax.ppermute(first, dp_axes, [(t, s) for s, t in to_same])
    second = lax.ppermute(second, dp_axes, [(t, s) for s, t in to_other])
    grad_out = jnp.where(odd == 0, jnp.stack([first, second], 1), jnp.stack([second, first], 1))
    grad_gate = (
        g_gate.reshape(TP, 2, rows, 2, FF // TP).transpose(2, 1, 3, 0, 4).reshape(rows, 2, 2 * FF)
    )
    grad_down = g_down.reshape(TP, rows, D).transpose(1, 0, 2)
    grads = [grad_in, grad_out, grad_gate, grad_down]

    weights = (attend_in, attend_out, gate_up, down_proj)

    def to_blocks(array):
        k, columns = array.shape[1:]
        shaped = array.reshape(rows, k, columns // B, B).transpose(1, 2, 0, 3)
        return shaped.reshape(k * (columns // B), rows, B)

    squares = [
        jnp.sum((w * w).reshape(rows, w.shape[1], w.shape[2] // B, B), (0, 3)).reshape(-1)
        for w in weights
    ]
    sums = lax.psum(jnp.concatenate([gain_one, gain_two] + squares), ALL)
    gain_grads = sums[: 2 * D].reshape(2, D)
    weight_size = jnp.sqrt(sums[2 * D :] / (B * B) + STEP_EPS)

    total_slots = left_stats.shape[0] * devices
    owner = (block_slots[None, :] == jnp.arange(total_slots, dtype=jnp.int32)[:, None]).astype(BF)
    grad_blocks = jnp.concatenate([to_blocks(g) for g in grads], 0)
    send = jnp.einsum("sb,bxy->sxy", owner, grad_blocks, preferred_element_type=F32).astype(BF)
    owned = lax.all_to_all(send, ALL, split_axis=0, concat_axis=1, tiled=True)
    product = lambda spec, p, q: jnp.einsum(spec, p, q, preferred_element_type=F32)
    direction = product("sij,sjk->sik", left_roots.astype(BF), owned).astype(BF)
    direction = product("sij,sjk->sik", direction, right_inverse_roots.astype(BF))
    size = jnp.mean(direction * direction, (1, 2), keepdims=True)
    direction = (direction * lax.rsqrt(size + STEP_EPS)).astype(BF)
    returned = lax.all_to_all(direction, ALL, split_axis=1, concat_axis=0, tiled=True)
    left_new = STAT_DECAY * left_stats + (1.0 - STAT_DECAY) * product("sij,skj->sik", owned, owned)
    right_new = STAT_DECAY * right_stats + (1.0 - STAT_DECAY) * product("sji,sjk->sik", owned, owned)
    steps = jnp.einsum("sb,sxy->bxy", owner, returned, preferred_element_type=F32)
    steps = STEP_RATE * weight_size[:, None, None] * steps
    new_weights, offset = [], 0
    for w in weights:
        k, columns = w.shape[1:]
        count = k * (columns // B)
        step = steps[offset : offset + count].reshape(k, columns // B, rows, B)
        new_weights.append(w - step.transpose(2, 0, 1, 3).reshape(w.shape))
        offset += count
    return (
        layer_output,
        input_grad,
        *[g.astype(F32) for g in grads],
        gain_grads,
        *new_weights,
        norm_gains - GAIN_RATE * gain_grads,
        left_new,
        right_new,
    )


def solution(mesh):
    outer = mesh.shape["dp"] // TP
    fine = Mesh(mesh.devices.reshape(outer, 2, 2, 2, mesh.shape["seq"]), ALL)
    dp = ("o",) + TENSOR
    by_token = P(dp, "z", None)
    by_row = P(ALL, None, None)
    return jax.shard_map(
        on_device,
        mesh=fine,
        in_specs=(by_token,) * 2 + (by_row,) * 4 + (P(), P(dp), P()) + (by_row,) * 4,
        out_specs=(by_token,) * 2 + (by_row,) * 4 + (P(),) + (by_row,) * 4 + (P(),) + (by_row,) * 2,
        check_vma=False,
    )
```

time: 5620 us -> 1570 us (0.28)
  waiting for transfers between devices: 4650 us -> 648 us
  local copies, waits for them, and re-layouts: 453 us -> 236 us
  starting transfers between devices: 17.3 us -> 164 us
  matrix products: 341 us -> 217 us
  blocking collectives: 81 us -> 173 us
  other arithmetic: 44.9 us -> 108 us
    unnamed x15 -> x8, waiting for transfers between devices: 2370 us -> 1 us
    reduce_scatter x3 -> x4, waiting for transfers between devices: 1430 us -> 77.5 us  [the longest x3 47.4 us: to_owners(): grad = lax.psum_scatter(grad, SHARD, scatter_dimension=0, tiled=True)]
    all_gather x6 -> x4, waiting for transfers between devices: 772 us -> 58.6 us  [the longest x3 58.6 us: to_full(): every = lax.all_gather(parts, SHARD, axis=0, tiled=False)]
    ppermute x0 -> x88, waiting for transfers between devices: none -> 351 us  [the longest x84 347 us: flip(): return lax.ppermute(value, axis, [(0, 1), (1, 0)])]
    transpose x4 -> x8, local copies, waits for them, and re-layouts: 273 us -> 18.8 us  [the longest x3 15 us: to_full(): return every.transpose(3, 0, 2, 1, 4, 5).reshape(lead * B, columns)]
    dot_general x25 -> x37, matrix products: 341 us -> 217 us  [the longest x12 62.9 us: dot_nt(): lax.dot_general(x, y, (((1,), (1,)), ((), ())), preferred_element_type=F32)]
    ppermute x0 -> x88, starting transfers between devices: none -> 97.7 us  [the longest x84 88.8 us: flip(): return lax.ppermute(value, axis, [(0, 1), (1, 0)])]
    all_to_all x3 -> x15, waiting for transfers between devices: 81.9 us -> 160 us  [the longest x13 133 us: exchange(): return lax.all_to_all(value, axes, split_axis=0, concat_axis=0, tiled=True)]
  transfers between devices with their start and end apart: 15 -> 111, of which waited for: 11 -> 75; matrix products, arithmetic and copies ran while one was open for 11% -> 22% of each run, Pallas kernels for 0% -> 0%
where the time goes in v1:
time: 1570 us
  waiting for transfers between devices  648 us (41%)
  local copies, waits for them, and re-layouts  236 us (15%)
  matrix products  217 us (14%)
  blocking collectives  173 us (11%)
  starting transfers between devices  164 us (10%)
  other arithmetic  108 us (7%)
  between operations  18 us (1%)
    ppermute x84, waiting for transfers between devices, flip(): return lax.ppermute(value, axis, [(0, 1), (1, 0)])  347 us
    all_to_all x13, waiting for transfers between devices, exchange(): return lax.all_to_all(value, axes, split_axis=0, concat_axis=0, tiled=True)  133 us
    psum x1, blocking collectives, on_device(): sums = lax.psum(jnp.concatenate([gain_one, gain_two] + squares), ALL)  102 us
    ppermute x84, starting transfers between devices, flip(): return lax.ppermute(value, axis, [(0, 1), (1, 0)])  88.8 us
    unnamed x358, local copies, waits for them, and re-layouts  82.4 us
    all_to_all x2, blocking collectives, exchange(): return lax.all_to_all(value, axes, split_axis=0, concat_axis=0, tiled=True)  71.1 us
    dot_general x12, matrix products, dot_nt(): lax.dot_general(x, y, (((1,), (1,)), ((), ())), preferred_element_type=F32)  62.9 us
    dot_general x8, matrix products, dot_tn(): lax.dot_general(x, y, (((0,), (0,)), ((), ())), preferred_element_type=F32)  58.9 us
  transfers between devices with their start and end apart: 111, of which 75 were waited for; matrix products, arithmetic and copies ran while one was open for 22% of the time, Pallas kernels for 0%

profile of v1, /device:TPU:0, one launch (start us, length us, event | category | flops | bytes accessed | tf_op | source)
XLA Modules:
  0.0 1565.0 jit_solution(10937956947294195690)
XLA Ops:
  56.0 37.4 %all-to-all-done.1 = bf16[4,2,32,2048]{3,2,1,0:T(8,128)(2,1)S(1)} async-done(((bf16[4,2,32,2048]{3,2,1,0:T(8,128)(2,1)}), bf16[4,2,32,2048]{3,2,1,0:T(8,128)(2,1)S(1)}, u32[]{:S(2)}, u32[]{:S(2)}) %all-to-all-start.1) | async-done | bytes 1048608 | tf_op jit(solution)/shard_map/all_to_all | solution.py:91
  104.6 13.3 collective-permute-done
  220.7 14.8 all-to-all-done.8
  247.8 24.4 %all-to-all-done.9 = bf16[4,2,32,2048]{3,2,1,0:T(8,128)(2,1)S(1)} async-done(((bf16[4,2,32,2048]{3,2,1,0:T(8,128)(2,1)}), bf16[4,2,32,2048]{3,2,1,0:T(8,128)(2,1)S(1)}, u32[]{:S(2)}, u32[]{:S(2)}) %all-to-all-start.9) | async-done | bytes 1048608 | tf_op jit(solution)/shard_map/all_to_all | solution.py:91
  343.8 58.6 %all-gather.12.cloned.1.call-done = bf16[32,2,32,2048]{3,2,1,0:T(8,128)(2,1)} async-done(((bf16[8,2,32,2048]{3,2,1,0:T(8,128)(2,1)}), bf16[32,2,32,2048]{3,2,1,0:T(8,128)(2,1)}) %all-gather.12.cloned.1.call-update) | async-done | bytes 8388624 | tf_op jit(solution)/shard_map/all_gather | solution.py:181
  410.7 14.8 fusion.264
  436.9 12.6 fusion.42
  638.0 16.3 %collective-permute-done.65 = bf16[64,2048]{1,0:T(8,128)(2,1)S(1)} collective-permute-done((bf16[64,2048]{1,0:T(8,128)(2,1)S(1)}, bf16[64,2048]{1,0:T(8,128)(2,1)S(1)}, u32[]{:S(2)}, u32[]{:S(2)}) %collective-permute-start.65) | collective-permute-done | bytes 262176 | tf_op jit(solution)/shard_map/ppermute | solution.py:45
  660.0 12.2 collective-permute-done.33
  725.9 11.7 multiply_convert_fusion.3
  737.6 12.2 fusion.39
  759.2 11.9 collective-permute-done.71
  842.1 12.0 convolution_convert_fusion.6
  856.5 26.0 %fusion.8 = bf16[2048,2048]{1,0:T(8,128)(2,1)} fusion(bf16[2048,2048]{1,0:T(8,128)(2,1)} %get-tuple-element.192, bf16[1024,1024]{1,0:T(8,128)(2,1)} %get-tuple-element.141, bf16[1024,1024]{1,0:T(8,128)(2,1)} %get-tuple-element.140, bf16[1024,1024]{1,0:T(8,128)(2,1)} %get-tuple-element.139, bf16[1024,1024]{1,0:T(8,128)(2,1)S(1)} %copy-done.134), kind=kOutput, calls=%fused_computation.12 | convolution fusion | flops 17217617920 | bytes 25165824 | tf_op jit(solution)/shard_map/dot_general | solution.py:41
  952.2 57.2 %all_to_all.112 = bf16[4,2,32,2048]{3,2,1,0:T(8,128)(2,1)} all-to-all(bf16[4,2,32,2048]{3,2,1,0:T(8,128)(2,1)S(1)} %maximum_bitcast_fusion), channel_id=1, replica_groups=mesh['o'=1,'a'=2,'b'=2,'c'=2,'z'=4] {'z'}, dimensions={0} | all-to-all | bytes 2097152 | tf_op jit(solution)/shard_map/all_to_all | solution.py:91
  1028.4 13.9 all_to_all.113
  1042.3 47.4 %reduce-scatter.9.cloned.1.call-done = bf16[512,2048]{1,0:T(8,128)(2,1)} async-done(((bf16[2048,2048]{1,0:T(8,128)(2,1)}), bf16[512,2048]{1,0:T(8,128)(2,1)}) %reduce-scatter.9.cloned.1.call-update) | async-done | bytes 2097168 | tf_op jit(solution)/shard_map/reduce_scatter | solution.py:273
  1094.0 30.2 %reduce-scatter.7.cloned.1.call-done = bf16[1,2,32,2048]{3,2,1,0:T(8,128)(2,1)} async-done(((bf16[4,2,32,2048]{3,2,1,0:T(8,128)(2,1)}), bf16[1,2,32,2048]{3,2,1,0:T(8,128)(2,1)}) %reduce-scatter.7.cloned.1.call-update) | async-done | bytes 262160 | tf_op jit(solution)/shard_map/reduce_scatter | solution.py:287
  1193.6 34.7 %collective-permute-done.82 = bf16[128,2048]{1,0:T(8,128)(2,1)S(1)} collective-permute-done((bf16[128,2048]{1,0:T(8,128)(2,1)S(1)}, bf16[128,2048]{1,0:T(8,128)(2,1)S(1)}, u32[]{:S(2)}, u32[]{:S(2)}) %collective-permute-start.82) | collective-permute-done | bytes 524320 | tf_op jit(solution)/shard_map/ppermute | solution.py:45
  1245.5 27.2 %all-to-all-done.15 = bf16[64,32,1024]{2,1,0:T(8,128)(2,1)} async-done(((bf16[64,32,1024]{2,1,0:T(8,128)(2,1)}), bf16[64,32,1024]{2,1,0:T(8,128)(2,1)}, u32[]{:S(2)}, u32[]{:S(2)}) %all-to-all-start.15) | async-done | bytes 4194336 | tf_op jit(solution)/shard_map/all_to_all | solution.py:343
  1282.4 22.1 %all-to-all-done.10 = bf16[4,2,32,2048]{3,2,1,0:T(8,128)(2,1)} async-done(((bf16[4,2,32,2048]{3,2,1,0:T(8,128)(2,1)}), bf16[4,2,32,2048]{3,2,1,0:T(8,128)(2,1)}, u32[]{:S(2)}, u32[]{:S(2)}) %all-to-all-start.10) | async-done | bytes 1048608 | tf_op jit(solution)/shard_map/all_to_all | solution.py:91
  1309.2 16.3 %multiply_reduce_fusion = (f32[2]{0:T(128)S(1)}, f32[2,1024,1024]{2,1,0:T(8,128)}) fusion(f32[2,1024,1024]{2,1,0:T(8,128)} %param.25, bf16[2,1024,1024]{2,1,0:T(8,128)(2,1)} %bitcast.355, f32[2,1024,1024]{2,1,0:T(8,128)} %param.24), kind=kOutput, calls=%fused_computation.11 | convolution fusion | flops 8600420352 | bytes 29360136 | tf_op jit(solution)/shard_map/sij,sjk->sik/dot_general | solution.py:344
  1354.8 101.5 %psum.7 = f32[4156]{0:T(1024)S(1)} all-reduce(f32[4156]{0:T(1024)S(1)} %concatenate.431), channel_id=1, replica_groups=mesh['o'=1,'a'=2,'b'=2,'c'=2,'z'=4] {'o','a','b','c','z'}, use_global_device_ids=true, to_apply=%region_30.31 | all-reduce | flops 4156 | bytes 33248 | tf_op jit(solution)/shard_map/psum | solution.py:335
  1468.6 14.0 add_multiply_fusion
  (881 shorter events, 904.4 us)
Async XLA Ops:
  32.2 87.4 %collective-permute-start.6 = (bf16[32,2048]{1,0:T(8,128)(2,1)}, bf16[32,2048]{1,0:T(8,128)(2,1)S(1)}, u32[]{:S(2)}, u32[]{:S(2)}) collective-permute-start(bf16[32,2048]{1,0:T(8,128)(2,1)} %get-tuple-element.395), channel_id=1, source_target_pairs={{0,0},{4,16},{8,4},{12,20},{16,8},{20,24},{24,12},{28,28},{1,1},{5... | collective-permute-start | bytes 393224 | tf_op jit(solution)/shard_map/ppermute | solution.py:205
  33.7 85.8 %collective-permute-start.7 = (bf16[32,2048]{1,0:T(8,128)(2,1)S(1)}, bf16[32,2048]{1,0:T(8,128)(2,1)}, u32[]{:S(2)}, u32[]{:S(2)}) collective-permute-start(bf16[32,2048]{1,0:T(8,128)(2,1)S(1)} %get-tuple-element.396), channel_id=1, source_target_pairs={{0,16},{4,0},{8,20},{12,4},{16,24},{20,8},{24,28},{28,12},{1,17},{... | collective-permute-start | bytes 393224 | tf_op jit(solution)/shard_map/ppermute | solution.py:206
  47.8 45.5 %all-to-all-start.1 = ((bf16[4,2,32,2048]{3,2,1,0:T(8,128)(2,1)}), bf16[4,2,32,2048]{3,2,1,0:T(8,128)(2,1)S(1)}, u32[]{:S(2)}, u32[]{:S(2)}) async-start(bf16[4,2,32,2048]{3,2,1,0:T(8,128)(2,1)} %bitcast.360), calls=%async_computation.1 | async-start | bytes 2097152 | tf_op jit(solution)/shard_map/all_to_all | solution.py:91
  52.7 109.3 %all-gather.10.cloned.1.call-start = ((), (), s32[]{:S(2)}) async-start(), calls=%async_computation.26 | async-start | bytes 2621440 | tf_op jit(solution)/shard_map/all_gather | solution.py:181
  93.3 62.4 %all-to-all-start.5 = ((bf16[8,32,2048]{2,1,0:T(8,128)(2,1)}), bf16[8,32,2048]{2,1,0:T(8,128)(2,1)}, u32[]{:S(2)}, u32[]{:S(2)}) async-start(bf16[8,32,2048]{2,1,0:T(8,128)(2,1)} %bitcast.299), calls=%async_computation.5 | async-start | bytes 2097152 | tf_op jit(solution)/shard_map/all_to_all | solution.py:91
  97.8 93.8 %all-gather.8.cloned.1.call-start = ((), (), s32[]{:S(2)}) async-start(), calls=%async_computation.21 | async-start | bytes 1310720 | tf_op jit(solution)/shard_map/all_gather | solution.py:208
  159.7 175.2 %all-gather.14.cloned.1.call-start = ((), (), s32[]{:S(2)}) async-start(), calls=%async_computation.28 | async-start | bytes 5242880 | tf_op jit(solution)/shard_map/all_gather | solution.py:181
  207.6 32.8 %collective-permute-start.8 = (bf16[512,2048]{1,0:T(8,128)(2,1)}, bf16[512,2048]{1,0:T(8,128)(2,1)}, u32[]{:S(2)}, u32[]{:S(2)}) collective-permute-start(bf16[512,2048]{1,0:T(8,128)(2,1)} %slice.873), channel_id=1, source_target_pairs={{0,4},{4,0},{1,5},{5,1},{2,6},{6,2},{3,7},{7,3},{8,12},{12,8},{9,1... | collective-permute-start | bytes 6291464 | tf_op jit(solution)/shard_map/ppermute | solution.py:45
  220.1 182.3 %all-gather.12.cloned.1.call-start = ((), (), s32[]{:S(2)}) async-start(), calls=%async_computation.27 | async-start | bytes 10485760 | tf_op jit(solution)/shard_map/all_gather | solution.py:181
  235.5 36.7 %all-to-all-start.9 = ((bf16[4,2,32,2048]{3,2,1,0:T(8,128)(2,1)}), bf16[4,2,32,2048]{3,2,1,0:T(8,128)(2,1)S(1)}, u32[]{:S(2)}, u32[]{:S(2)}) async-start(bf16[4,2,32,2048]{3,2,1,0:T(8,128)(2,1)} %bitcast.54), calls=%async_computation.9 | async-start | bytes 2097152 | tf_op jit(solution)/shard_map/all_to_all | solution.py:91
  240.4 769.1 %reduce-scatter.11.cloned.1.call-start = ((), (), s32[]{:S(2)}) async-start(), calls=%async_computation.25 | async-start | bytes 5242880 | tf_op jit(solution)/shard_map/reduce_scatter | solution.py:273
  246.7 34.8 %collective-permute-start.9 = (bf16[128,2048]{1,0:T(8,128)(2,1)}, bf16[128,2048]{1,0:T(8,128)(2,1)S(1)}, u32[]{:S(2)}, u32[]{:S(2)}) collective-permute-start(bf16[128,2048]{1,0:T(8,128)(2,1)} %get-tuple-element.214), channel_id=1, source_target_pairs={{0,16},{16,0},{1,17},{17,1},{2,18},{18,2},{3,19},{19,3},{4,20},{20... | collective-permute-start | bytes 1572872 | tf_op jit(solution)/shard_map/ppermute | solution.py:45
  247.2 34.3 %collective-permute-start.11 = (bf16[128,2048]{1,0:T(8,128)(2,1)}, bf16[128,2048]{1,0:T(8,128)(2,1)S(1)}, u32[]{:S(2)}, u32[]{:S(2)}) collective-permute-start(bf16[128,2048]{1,0:T(8,128)(2,1)} %get-tuple-element.215), channel_id=1, source_target_pairs={{0,8},{8,0},{1,9},{9,1},{2,10},{10,2},{3,11},{11,3},{4,12},{12,4},... | collective-permute-start | bytes 1572872 | tf_op jit(solution)/shard_map/ppermute | solution.py:45
  636.4 45.0 %collective-permute-start.68 = (bf16[128,2048]{1,0:T(8,128)(2,1)S(1)}, bf16[128,2048]{1,0:T(8,128)(2,1)S(1)}, u32[]{:S(2)}, u32[]{:S(2)}) collective-permute-start(bf16[128,2048]{1,0:T(8,128)(2,1)S(1)} %pad_maximum_fusion.21), channel_id=1, source_target_pairs={{0,8},{8,0},{1,9},{9,1},{2,10},{10,2},{3,11},{11,3},{4,12},{12,4},... | collective-permute-start | bytes 1572872 | tf_op jit(solution)/shard_map/ppermute | solution.py:45
  804.2 224.2 %reduce-scatter.5.cloned.1.call-start = ((), (), s32[]{:S(2)}) async-start(), calls=%async_computation.22 | async-start | bytes 2621440 | tf_op jit(solution)/shard_map/reduce_scatter | solution.py:273
  855.6 234.0 %reduce-scatter.9.cloned.1.call-start = ((), (), s32[]{:S(2)}) async-start(), calls=%async_computation.24 | async-start | bytes 10485760 | tf_op jit(solution)/shard_map/reduce_scatter | solution.py:273
  1013.0 111.1 %reduce-scatter.7.cloned.1.call-start = ((), (), s32[]{:S(2)}) async-start(), calls=%async_computation.23 | async-start | bytes 1310720 | tf_op jit(solution)/shard_map/reduce_scatter | solution.py:287
  1089.6 61.1 %all-to-all-start.13 = ((bf16[8,2,32,2048]{3,2,1,0:T(8,128)(2,1)}), bf16[8,2,32,2048]{3,2,1,0:T(8,128)(2,1)}, u32[]{:S(2)}, u32[]{:S(2)}) async-start(bf16[8,2,32,2048]{3,2,1,0:T(8,128)(2,1)} %bitcast.383), calls=%async_computation.16 | async-start | bytes 4194304 | tf_op jit(solution)/shard_map/all_to_all | solution.py:91
  1176.5 96.2 %all-to-all-start.15 = ((bf16[64,32,1024]{2,1,0:T(8,128)(2,1)}), bf16[64,32,1024]{2,1,0:T(8,128)(2,1)}, u32[]{:S(2)}, u32[]{:S(2)}) async-start(bf16[64,32,1024]{2,1,0:T(8,128)(2,1)} %copy.407), calls=%async_computation.19 | async-start | bytes 8388608 | tf_op jit(solution)/shard_map/all_to_all | solution.py:343
  1190.3 37.9 %collective-permute-start.82 = (bf16[128,2048]{1,0:T(8,128)(2,1)S(1)}, bf16[128,2048]{1,0:T(8,128)(2,1)S(1)}, u32[]{:S(2)}, u32[]{:S(2)}) collective-permute-start(bf16[128,2048]{1,0:T(8,128)(2,1)S(1)} %get-tuple-element.208), channel_id=1, source_target_pairs={{0,16},{16,0},{1,17},{17,1},{2,18},{18,2},{3,19},{19,3},{4,20},{20... | collective-permute-start | bytes 1572872 | tf_op jit(solution)/shard_map/ppermute | solution.py:45
  1192.2 37.1 %collective-permute-start.84 = (bf16[128,2048]{1,0:T(8,128)(2,1)S(1)}, bf16[128,2048]{1,0:T(8,128)(2,1)S(1)}, u32[]{:S(2)}, u32[]{:S(2)}) collective-permute-start(bf16[128,2048]{1,0:T(8,128)(2,1)S(1)} %get-tuple-element.209), channel_id=1, source_target_pairs={{0,8},{8,0},{1,9},{9,1},{2,10},{10,2},{3,11},{11,3},{4,12},{12,4},... | collective-permute-start | bytes 1572872 | tf_op jit(solution)/shard_map/ppermute | solution.py:45
  1272.7 31.8 %all-to-all-start.10 = ((bf16[4,2,32,2048]{3,2,1,0:T(8,128)(2,1)}), bf16[4,2,32,2048]{3,2,1,0:T(8,128)(2,1)}, u32[]{:S(2)}, u32[]{:S(2)}) async-start(bf16[4,2,32,2048]{3,2,1,0:T(8,128)(2,1)} %maximum_bitcast_fusion.1), calls=%async_computation.10 | async-start | bytes 2097152 | tf_op jit(solution)/shard_map/all_to_all | solution.py:91
  1304.5 32.0 %all-to-all-start.11 = ((bf16[8,1,32,2048]{3,2,1,0:T(8,128)(2,1)}), bf16[8,1,32,2048]{3,2,1,0:T(8,128)(2,1)}, u32[]{:S(2)}, u32[]{:S(2)}) async-start(bf16[8,1,32,2048]{3,2,1,0:T(8,128)(2,1)} %bitcast.78), calls=%async_computation.11 | async-start | bytes 2097152 | tf_op jit(solution)/shard_map/all_to_all | solution.py:91
  1336.5 155.3 %all-to-all-start.16 = ((bf16[2,1024,1024]{2,0,1:T(2,128)(2,1)}), bf16[2,1024,1024]{2,0,1:T(2,128)(2,1)}, u32[]{:S(2)}, u32[]{:S(2)}) async-start(bf16[2,1024,1024]{2,0,1:T(2,128)(2,1)} %copy.411), calls=%async_computation.20 | async-start | bytes 8388608 | tf_op jit(solution)/shard_map/all_to_all | solution.py:349
  (228 other events, 4075.4 us)
Sparse Core Ops, SparseCore 0:
  56.1 53.7 all-gather.9
  121.4 27.0 all-gather.7
  162.1 89.9 all-gather.13
  254.1 148.2 all-gather.11
  804.3 75.1 reduce-scatter.10
  881.7 44.3 reduce-scatter.4
  929.0 160.5 reduce-scatter.8
  1092.5 31.6 reduce-scatter.6

commit v2 on v1

v2 whole, which is shorter than its diff:
```python
import functools

import jax
import jax.numpy as jnp
from jax import lax
from jax.experimental import pallas as pl
from jax.experimental.pallas import tpu as pltpu
from jax.sharding import Mesh
from jax.sharding import PartitionSpec as P

D = 2048
HEADS = 8
KV_HEADS = 4
HEAD = 256
FF = 8192
B = 1024
QD = 2048
KVD = 1024
TP = 8
UNITS = FF // TP

NORM_EPS = 1e-06
ROPE_BASE = 1000042.0
STAT_DECAY = 0.5
STEP_RATE = 0.5
GAIN_RATE = 0.002
STEP_EPS = 1e-06
MASKED = -1e30
VMEM_BYTES = 48 * 1024 * 1024

BF = jnp.bfloat16
F32 = jnp.float32
TENSOR = ("a", "b", "c")
SHARD = ("o", "z")
ALL = ("o", "a", "b", "c", "z")


def dot(x, y, out=F32):
    return lax.dot_general(x, y, (((1,), (0,)), ((), ())), preferred_element_type=F32).astype(out)


def dot_nt(x, y, out=F32):
    return lax.dot_general(x, y, (((1,), (1,)), ((), ())), preferred_element_type=F32).astype(out)


def dot_tn(x, y, out=F32):
    return lax.dot_general(x, y, (((0,), (0,)), ((), ())), preferred_element_type=F32).astype(out)


def flip(value, axis):
    return lax.ppermute(value, axis, [(0, 1), (1, 0)])


def after(value, *others):
    return pl.pallas_call(
        lambda *refs: None,
        in_specs=[pl.BlockSpec(memory_space=pl.ANY)] * (1 + len(others)),
        out_specs=pl.BlockSpec(memory_space=pl.ANY),
        out_shape=jax.ShapeDtypeStruct(value.shape, value.dtype),
        input_output_aliases={0: 0},
        name="after",
    )(value, *others)


def assemble(pieces):
    arrays, places = [], []
    for array, start, count in pieces:
        if not any(array is other for other in arrays):
            arrays.append(array)
        index = [array is other for other in arrays].index(True)
        places.append((index, start, count))
    total = sum(count for _, _, count in places)

    def kernel(*refs):
        sources, out, sems = refs[: len(arrays)], refs[-2], refs[-1]
        copies, row = [], 0
        for i, (index, start, count) in enumerate(places):
            copies.append(
                pltpu.make_async_copy(
                    sources[index].at[pl.ds(start, count)], out.at[pl.ds(row, count)], sems.at[i]
                )
            )
            copies[-1].start()
            row += count
        for copy in copies:
            copy.wait()

    return pl.pallas_call(
        kernel,
        in_specs=[pl.BlockSpec(memory_space=pl.ANY)] * len(arrays),
        out_specs=pl.BlockSpec(memory_space=pltpu.VMEM),
        out_shape=jax.ShapeDtypeStruct((total, arrays[0].shape[1]), arrays[0].dtype),
        scratch_shapes=[pltpu.SemaphoreType.DMA((len(places),))],
        compiler_params=pltpu.CompilerParams(vmem_limit_bytes=VMEM_BYTES),
        cost_estimate=pl.CostEstimate(
            flops=0, bytes_accessed=4 * total * arrays[0].shape[1], transcendentals=0
        ),
        name="assemble",
    )(*arrays)


ORDER_P = (0, 2, 4, 6, 1, 3, 5, 7)
ORDER_Q = (0, 4, 2, 6, 1, 5, 3, 7)


def gather_tokens(value, middle=(), end=()):
    h = value.shape[0] // 2
    by_b, by_a, by_c = flip(value, "b"), flip(value, "a"), flip(value, "c")
    p_b, q_a = by_b[:h], by_a[h:]
    if middle:
        p_b, q_a = after(p_b, *middle), after(q_a, *middle)
    p_ab = flip(p_b, "a")
    q_ab = flip(q_a, "b")
    by_bc, by_ac = flip(by_b, "c"), flip(by_a, "c")
    p_abc, q_abc = flip(p_ab, "c"), flip(q_ab, "c")
    if end:
        p_abc = after(p_abc, *end)
    return assemble(
        [(t, 0, h) for t in (value, by_b, by_a, p_ab, by_c, by_bc, by_ac, p_abc)]
        + [(t, h, h) for t in (value, by_a, by_b)]
        + [(q_ab, 0, h)]
        + [(t, h, h) for t in (by_c, by_ac, by_bc)]
        + [(q_abc, 0, h)]
    )


def scatter_tokens(rows, times, middle=(), end=()):
    quarter = rows.shape[0] // 4
    p_far = flip(times(rows[quarter : 2 * quarter]).astype(BF), "c")
    q_far = flip(times(rows[3 * quarter :]).astype(BF), "c")
    p = times(rows[:quarter]) + p_far.astype(F32)
    q = times(rows[2 * quarter : 3 * quarter]) + q_far.astype(F32)
    e = quarter // 2
    p_got = flip(p[e:].astype(BF), "a")
    q_got = flip(q[e:].astype(BF), "b")
    if middle:
        p_got, q_got = after(p_got, *middle), after(q_got, *middle)
    p_sum = p[:e] + p_got.astype(F32)
    q_sum = q[:e] + q_got.astype(F32)
    f = e // 2
    p_got = flip(p_sum[f:].astype(BF), "b")
    q_got = flip(q_sum[f:].astype(BF), "a")
    if end:
        p_got, q_got = after(p_got, *end), after(q_got, *end)
    return jnp.concatenate([p_sum[:f] + p_got.astype(F32), q_sum[:f] + q_got.astype(F32)], 0)


def sum_everywhere(value):
    for axis in ALL:
        count = lax.axis_size(axis)
        bit = 1
        while bit < count:
            value = value + lax.ppermute(value, axis, [(i, i ^ bit) for i in range(count)])
            bit *= 2
    return value


def swap_halves(value):
    half = value.shape[1] // 2
    return jnp.concatenate([value[:, half:], value[:, :half]], 1)


def exchange(value, axes):
    return lax.all_to_all(value, axes, split_axis=0, concat_axis=0, tiled=True)


def share_tokens(tokens):
    seqs, length, width = tokens.shape
    n = length // TP
    parts = tokens.reshape(seqs, TP, n, width).transpose(1, 0, 2, 3)
    return parts.reshape(TP * seqs, n, width)


def swap_z(value, z_count):
    z = lax.axis_index("z")
    parts = [lax.dynamic_index_in_dim(value, z ^ i, 0, keepdims=False) for i in range(z_count)]
    return [
        parts[i] if i == 0 else lax.ppermute(parts[i], "z", [(j, j ^ i) for j in range(z_count)])
        for i in range(z_count)
    ]


def reshard(parts, z_count):
    every, n, width = parts.shape
    m = every // z_count
    parts = swap_z(parts.reshape(z_count, m * n, width), z_count)
    return jnp.concatenate([part[s * n : (s + 1) * n] for s in range(m) for part in parts], 0)


def reshard_back(values, z_count, seqs):
    m = TP * seqs // z_count
    n = values.shape[0] // (m * z_count)
    width = values.shape[1]
    z = lax.axis_index("z")
    parts = values.reshape(m, z_count, n, width).transpose(1, 0, 2, 3).reshape(z_count, m * n, width)
    out = jnp.zeros_like(parts)
    for i in range(z_count):
        part = parts[i]
        if i > 0:
            part = lax.ppermute(part, "z", [(j, j ^ i) for j in range(z_count)])
        out = lax.dynamic_update_index_in_dim(out, part, z ^ i, 0)
    parts = exchange(out.reshape(TP, seqs, n, width), TENSOR)
    return parts.transpose(1, 0, 2, 3).reshape(seqs, TP * n, width)


def rms_scale(value):
    return lax.rsqrt(jnp.mean(value * value, -1, keepdims=True) + NORM_EPS)


def norm_back(value, scaler, gain, upstream):
    weighted = upstream * gain
    inner_mean = jnp.mean(weighted * value, -1, keepdims=True)
    return (
        scaler * weighted - value * scaler**3 * inner_mean,
        jnp.sum(upstream * value * scaler, 0),
    )


def rotate(value, cosine, sine):
    front, back = value[..., : HEAD // 2], value[..., HEAD // 2 :]
    return jnp.concatenate([front * cosine - back * sine, back * cosine + front * sine], -1)


def attend_kernel(limit, place, query, key, value, out, log_total):
    scores = dot_nt(query[0], key[0]) * HEAD ** (-0.5)
    scores = jnp.where(place[0] <= limit[0], scores, MASKED)
    top = jnp.max(scores, -1, keepdims=True)
    shifted = jnp.exp(scores - top)
    mass = jnp.sum(shifted, -1, keepdims=True)
    out[0] = dot((shifted / mass).astype(BF), value[0], BF)
    log_total[0] = top + jnp.log(mass)


def attend_back_kernel(
    limit, place, query, key, value, log_total, out_grad, query_grad, key_grad, value_grad
):
    @pl.when(pl.program_id(1) == 0)
    def _():
        key_grad[...] = jnp.zeros_like(key_grad)
        value_grad[...] = jnp.zeros_like(value_grad)

    scores = dot_nt(query[0], key[0]) * HEAD ** (-0.5)
    scores = jnp.where(place[0] <= limit[0], scores, MASKED)
    shares = jnp.exp(scores - log_total[0])
    share_grad = dot_nt(out_grad[0], value[0])
    inner = jnp.sum(shares * share_grad, -1, keepdims=True)
    score_grad = (shares * (share_grad - inner)).astype(BF)
    query_grad[0] = dot(score_grad, key[0]) * HEAD ** (-0.5)
    key_grad[0] += dot_tn(score_grad, query[0]) * HEAD ** (-0.5)
    value_grad[0] += dot_tn(shares.astype(BF), out_grad[0])


def attention_specs(length, block):
    by_query = lambda width: pl.BlockSpec((1, block, width), lambda s, i: (s, i, 0))
    whole = lambda width: pl.BlockSpec((1, length, width), lambda s, i: (s, 0, 0))
    return by_query, whole, pl.BlockSpec((1, 1, length), lambda s, i: (s, 0, 0))


def attend(limit, place, query, key, value):
    m, length = query.shape[:2]
    block = min(256, length)
    by_query, whole, row = attention_specs(length, block)
    return pl.pallas_call(
        attend_kernel,
        grid=(m, length // block),
        in_specs=[by_query(1), row, by_query(HEAD), whole(HEAD), whole(HEAD)],
        out_specs=[by_query(HEAD), by_query(1)],
        out_shape=[
            jax.ShapeDtypeStruct((m, length, HEAD), BF),
            jax.ShapeDtypeStruct((m, length, 1), F32),
        ],
        compiler_params=pltpu.CompilerParams(vmem_limit_bytes=VMEM_BYTES),
        cost_estimate=pl.CostEstimate(
            flops=4 * m * length * length * HEAD,
            bytes_accessed=m * length * HEAD * 8,
            transcendentals=m * length * length,
        ),
        name="attend",
    )(limit, place, query, key, value)


def attend_back(limit, place, query, key, value, log_total, out_grad):
    m, length = query.shape[:2]
    block = min(256, length)
    by_query, whole, row = attention_specs(length, block)
    return pl.pallas_call(
        attend_back_kernel,
        grid=(m, length // block),
        in_specs=[
            by_query(1), row, by_query(HEAD), whole(HEAD), whole(HEAD), by_query(1), by_query(HEAD),
        ],
        out_specs=[by_query(HEAD), whole(HEAD), whole(HEAD)],
        out_shape=[jax.ShapeDtypeStruct((m, length, HEAD), F32)] * 3,
        compiler_params=pltpu.CompilerParams(vmem_limit_bytes=VMEM_BYTES),
        cost_estimate=pl.CostEstimate(
            flops=10 * m * length * length * HEAD,
            bytes_accessed=m * length * HEAD * 20,
            transcendentals=m * length * length,
        ),
        name="attend_back",
    )(limit, place, query, key, value, log_total, out_grad)


def gate_kernel(rows, weight, hidden, gate_slope, up_slope):
    gate = dot(rows[...], weight[:, :UNITS])
    up = dot(rows[...], weight[:, UNITS:])
    sigmoid = jax.nn.sigmoid(gate)
    hidden[...] = (gate * sigmoid * up).astype(BF)
    gate_slope[...] = up * sigmoid * (1.0 + gate * (1.0 - sigmoid))
    up_slope[...] = gate * sigmoid


def gate_forward(rows, weight):
    count, block = rows.shape[0], 256
    by_row = lambda width: pl.BlockSpec((block, width), lambda i: (i, 0))
    return pl.pallas_call(
        gate_kernel,
        grid=(count // block,),
        in_specs=[by_row(D), pl.BlockSpec((D, 2 * UNITS), lambda i: (0, 0))],
        out_specs=[by_row(UNITS)] * 3,
        out_shape=[jax.ShapeDtypeStruct((count, UNITS), t) for t in (BF, F32, F32)],
        compiler_params=pltpu.CompilerParams(vmem_limit_bytes=VMEM_BYTES),
        cost_estimate=pl.CostEstimate(
            flops=4 * count * D * UNITS,
            bytes_accessed=2 * (count * D + 2 * D * UNITS) + 10 * count * UNITS,
            transcendentals=count * UNITS,
        ),
        name="gate_forward",
    )(rows, weight)


def gate_back_kernel(rows, weight, gate_slope, up_slope, out):
    hidden_grad = dot_nt(rows[...], weight[...])
    out[:, :UNITS] = (hidden_grad * gate_slope[...]).astype(BF)
    out[:, UNITS:] = (hidden_grad * up_slope[...]).astype(BF)


def gate_back(rows, weight, gate_slope, up_slope):
    count, block = rows.shape[0], 256
    by_row = lambda width: pl.BlockSpec((block, width), lambda i: (i, 0))
    return pl.pallas_call(
        gate_back_kernel,
        grid=(count // block,),
        in_specs=[by_row(D), pl.BlockSpec((UNITS, D), lambda i: (0, 0)), by_row(UNITS), by_row(UNITS)],
        out_specs=by_row(2 * UNITS),
        out_shape=jax.ShapeDtypeStruct((count, 2 * UNITS), BF),
        compiler_params=pltpu.CompilerParams(vmem_limit_bytes=VMEM_BYTES),
        cost_estimate=pl.CostEstimate(
            flops=2 * count * D * UNITS,
            bytes_accessed=2 * (count * D + D * UNITS) + 12 * count * UNITS,
            transcendentals=0,
        ),
        name="gate_back",
    )(rows, weight, gate_slope, up_slope)


def update_kernel(parts, slots, sizes, weight, *refs):
    out = refs[-1]
    column = pl.program_id(0)
    count = pl.num_programs(0)
    for k in range(parts):
        block = k * count + column
        even, odd = refs[2 * k][0].astype(F32), refs[2 * k + 1][0].astype(F32)
        step = jnp.where(slots[block] % 2 == 0, even, odd)
        out[:, k, :] = weight[:, k, :] - sizes[block] * step


def update(weight, slots, sizes, even, odd):
    rows, parts, columns = weight.shape
    count = columns // B
    step_spec = lambda k: pl.BlockSpec(
        (1, rows, B), lambda i, slots, sizes: (slots[k * count + i] // 2, 0, 0)
    )
    weight_spec = pl.BlockSpec((rows, parts, B), lambda i, slots, sizes: (0, 0, i))
    return pl.pallas_call(
        functools.partial(update_kernel, parts),
        grid_spec=pltpu.PrefetchScalarGridSpec(
            num_scalar_prefetch=2,
            grid=(count,),
            in_specs=[weight_spec] + [step_spec(k) for k in range(parts) for _ in range(2)],
            out_specs=weight_spec,
        ),
        out_shape=jax.ShapeDtypeStruct(weight.shape, F32),
        compiler_params=pltpu.CompilerParams(vmem_limit_bytes=VMEM_BYTES),
        name="update",
    )(slots, sizes, weight, *([even, odd] * parts))


def on_device(
    tokens,
    cotangent,
    attend_in,
    attend_out,
    gate_up,
    down_proj,
    norm_gains,
    prefix_lengths,
    block_slots,
    left_stats,
    right_stats,
    left_roots,
    right_inverse_roots,
):
    outer, z_count = lax.axis_size("o"), lax.axis_size("z")
    shards = outer * z_count
    devices = shards * TP
    rank = lax.axis_index(TENSOR)
    core = lax.axis_index("c")
    z_rank = lax.axis_index("z")
    seqs, z_tokens, width = tokens.shape
    n = z_tokens // TP
    m = TP * seqs // z_count
    if m != 2:
        raise ValueError(m)
    length = z_count * z_tokens
    rows = attend_in.shape[0]

    def to_full(every, lead):
        columns = every.shape[-1]
        every = every.reshape(outer, z_count, TP, lead, rows, columns)
        return every.transpose(3, 0, 2, 1, 4, 5).reshape(lead * B, columns)

    low_in = attend_in.astype(BF)
    heads = low_in[:, :, :QD].reshape(rows, 2, HEADS, HEAD)
    keys_values = low_in[:, :, QD:].reshape(rows, 2, 2, KV_HEADS, HEAD).transpose(0, 1, 3, 2, 4)
    mixed_cols = jnp.concatenate([heads, keys_values.reshape(rows, 2, HEADS, HEAD)], -1)
    mixed_cols = exchange(mixed_cols.transpose(2, 1, 0, 3), TENSOR)

    low_out = attend_out.astype(BF).transpose(1, 0, 2)
    holders = range(outer * TP)
    span = 2 * outer

    def home(g, k):
        return (g % span) // 2 * TP + g // span + 4 * k

    to_same = [(g, home(g, g % 2)) for g in holders]
    to_other = [(g, home(g, 1 - g % 2)) for g in holders]
    dp_axes = ("o",) + TENSOR
    odd = lax.axis_index(dp_axes) % 2
    upper = rank // 4
    same = jnp.where(odd == 0, low_out[0], low_out[1])
    other = jnp.where(odd == 0, low_out[1], low_out[0])
    same = lax.ppermute(same, dp_axes, to_same)
    other = lax.ppermute(other, dp_axes, to_other)
    pair = jnp.where(upper == 0, jnp.stack([same, other]), jnp.stack([other, same]))
    mix_rows = TP * 2 * rows
    quarters = pair.reshape(2, rows, 4, D // 4).transpose(2, 0, 1, 3).reshape(8 * rows, D // 4)
    joined_in = jnp.concatenate([mixed_cols.reshape(mix_rows, 2 * HEAD), quarters], 0)
    joined = lax.all_gather(joined_in, SHARD, axis=0, tiled=False)
    w_mix = joined[:, :mix_rows].reshape(outer, z_count, TP, 2, rows, 2 * HEAD)
    w_mix = w_mix.transpose(3, 0, 2, 1, 4, 5).reshape(D, 2 * HEAD)
    w_out = joined[:, mix_rows:].reshape(outer, z_count, 4, 2, rows, D // 4)
    w_out = w_out.transpose(0, 3, 1, 4, 2, 5).reshape(HEAD, D)

    x_parts = exchange(after(share_tokens(tokens), joined_in), TENSOR)
    x = reshard(x_parts, z_count).astype(F32)

    cut_gate = gate_up.astype(BF).reshape(rows, 2, 2, TP, UNITS).transpose(3, 1, 0, 2, 4)
    cut_gate = after(cut_gate.reshape(TP, 2, rows, 2 * UNITS), x_parts)
    cut_gate = exchange(cut_gate, TENSOR)
    every_gate = lax.all_gather(cut_gate, SHARD, axis=0, tiled=False)
    w_gate = to_full(every_gate, 2)

    def positions_of(order):
        base = (rank ^ jnp.array(order, jnp.int32)) * n
        quarters = (z_rank ^ jnp.arange(z_count, dtype=jnp.int32)) * z_tokens
        inner = jnp.arange(n, dtype=jnp.int32)
        return (base[:, None, None] + quarters[None, :, None] + inner[None, None, :]).reshape(-1)

    positions = jnp.stack([positions_of(ORDER_P), positions_of(ORDER_Q)])
    frequency = ROPE_BASE ** (-2.0 * jnp.arange(HEAD // 2, dtype=F32) / HEAD)
    angles = positions.astype(F32)[:, :, None] * frequency
    cosine, sine = jnp.cos(angles), jnp.sin(angles)
    prefixes = exchange(jnp.broadcast_to(prefix_lengths[None], (TP, seqs)), TENSOR).reshape(-1)
    prefixes = lax.dynamic_slice_in_dim(prefixes, z_rank * m, m)
    limit = jnp.maximum(positions, prefixes[:, None] - 1)[:, :, None]
    place = positions[:, None, :]

    scale_one = rms_scale(x)
    normed_one = (x * scale_one * norm_gains[0]).astype(BF)
    normed_one = gather_tokens(normed_one, middle=(joined,), end=(cut_gate,))
    cut_down = exchange(after(down_proj.astype(BF).transpose(1, 0, 2), normed_one), TENSOR)
    down_parts = exchange(after(share_tokens(cotangent), cut_gate), TENSOR)
    mixed = dot(normed_one, w_mix).reshape(m, length, 2 * HEAD)
    query = rotate(mixed[..., :HEAD], cosine, sine).astype(BF)
    own = mixed[..., HEAD:]
    own = jnp.where(core == 0, rotate(own, cosine, sine), own).astype(BF)
    got = swap_halves(flip(own, "c"))
    key = jnp.where(core == 0, own, got)
    value = jnp.where(core == 0, got, own)
    attended, log_total = attend(limit, place, query, key, value)
    attended = after(attended.reshape(m * length, HEAD), cut_down, down_parts)
    down_in = reshard(after(down_parts, attended), z_count)
    every_down = lax.all_gather(after(cut_down, every_gate), SHARD, axis=0, tiled=False)
    w_down = to_full(every_down, 1)
    middle = x + scatter_tokens(attended, lambda part: dot(part, w_out))
    scale_two = rms_scale(middle)
    normed_two = (middle * scale_two * norm_gains[1]).astype(BF)
    normed_two = gather_tokens(normed_two, middle=(down_in, every_gate))
    down_in = after(down_in, normed_two)
    hidden, gate_slope, up_slope = gate_forward(normed_two, w_gate)

    def by_shard(grad, lead):
        columns = grad.shape[-1]
        grad = grad.reshape(lead, outer, TP, z_count, rows, columns).transpose(1, 3, 2, 0, 4, 5)
        return grad.reshape(shards * TP * lead * rows, columns)

    def to_owners(grad):
        return lax.psum_scatter(grad, SHARD, scatter_dimension=0, tiled=True)

    upstream = gather_tokens(down_in, middle=(hidden,))
    g_down = by_shard(dot_tn(hidden, upstream, BF), 1)
    gate_rows = gate_back(after(upstream, g_down), w_down, gate_slope, up_slope)
    g_gate_raw = dot_tn(normed_two, gate_rows, BF)
    g_gate = by_shard(g_gate_raw, 2)
    normed_grad = scatter_tokens(
        gate_rows, lambda part: dot_nt(part, w_gate), middle=(g_gate_raw,), end=(g_gate,)
    )
    middle_grad, gain_two = norm_back(middle, scale_two, norm_gains[1], normed_grad)
    middle_grad = middle_grad + down_in.astype(F32)
    g_down = to_owners(g_down)
    g_gate = to_owners(g_gate)
    branch = gather_tokens(middle_grad.astype(BF), middle=(g_down,))
    g_down = exchange(g_down.reshape(TP, 1, rows, D), TENSOR)
    layer_out = middle + scatter_tokens(after(hidden, branch), lambda part: dot(part, w_down))
    layer_output = reshard_back(layer_out.astype(BF), z_count, seqs)
    attended_grad = dot_nt(branch, w_out, BF).reshape(m, length, HEAD)
    query_grad, key_grad, value_grad = attend_back(
        limit, place, query, key, value, log_total, attended_grad
    )
    keep = jnp.where(core == 0, key_grad, value_grad)
    give = jnp.where(core == 0, value_grad, key_grad)
    keep = keep + swap_halves(flip(give, "c"))
    keep = jnp.where(core == 0, rotate(keep, cosine, -sine), keep)
    mixed_grad = jnp.concatenate([rotate(query_grad, cosine, -sine), keep], -1).astype(BF)
    mixed_grad = mixed_grad.reshape(m * length, 2 * HEAD)

    g_mix = dot_tn(normed_one, mixed_grad, BF)
    g_out = dot_tn(attended, branch, BF)
    g_mix = g_mix.reshape(2, outer, TP, z_count, rows, 2 * HEAD).transpose(1, 3, 2, 0, 4, 5)
    g_out = g_out.reshape(outer, 2, z_count, rows, 4, D // 4).transpose(0, 2, 4, 1, 3, 5)
    joined = jnp.concatenate(
        [
            g_mix.reshape(shards, mix_rows, 2 * HEAD),
            g_out.reshape(shards, 8 * rows, D // 4),
        ],
        1,
    ).reshape(shards * (mix_rows + 8 * rows), 2 * HEAD)
    joined = to_owners(after(joined, g_gate, g_down))
    g_gate = exchange(g_gate.reshape(TP, 2, rows, 2 * UNITS), TENSOR)
    joined = after(joined, g_gate)
    g_mix = exchange(joined[:mix_rows].reshape(TP, 2, rows, 2 * HEAD), TENSOR)
    g_out = joined[mix_rows:].reshape(4, 2, rows, D // 4).transpose(1, 2, 0, 3).reshape(2, rows, D)

    normed_grad = scatter_tokens(mixed_grad, lambda part: dot_nt(part, w_mix), end=(g_gate,))
    input_grad, gain_one = norm_back(x, scale_one, norm_gains[0], normed_grad)
    input_grad = input_grad + middle_grad
    input_grad = after(input_grad.astype(BF), joined)
    input_grad = reshard_back(input_grad, z_count, seqs).astype(F32)

    weights = (attend_in, attend_out, gate_up, down_proj)
    squares = [
        jnp.sum((w * w).reshape(rows, w.shape[1], w.shape[2] // B, B), (0, 3)).reshape(-1)
        for w in weights
    ]
    sums = sum_everywhere(jnp.concatenate([gain_one, gain_two] + squares))
    gain_grads = sums[: 2 * D].reshape(2, D)
    weight_size = STEP_RATE * jnp.sqrt(sums[2 * D :] / (B * B) + STEP_EPS)

    g_heads = g_mix[..., :HEAD].transpose(2, 1, 0, 3).reshape(rows, 2, QD)
    g_kv = g_mix[..., HEAD:].reshape(KV_HEADS, 2, 2, rows, HEAD).transpose(3, 2, 1, 0, 4)
    grad_in = jnp.concatenate([g_heads, g_kv.reshape(rows, 2, 2 * KVD)], -1)
    first = jnp.where(upper == 0, g_out[0], g_out[1])
    second = jnp.where(upper == 0, g_out[1], g_out[0])
    first = lax.ppermute(first, dp_axes, [(t, s) for s, t in to_same])
    second = lax.ppermute(second, dp_axes, [(t, s) for s, t in to_other])
    grad_out = jnp.where(odd == 0, jnp.stack([first, second], 1), jnp.stack([second, first], 1))
    grad_gate = (
        g_gate.reshape(TP, 2, rows, 2, UNITS).transpose(2, 1, 3, 0, 4).reshape(rows, 2, 2 * FF)
    )
    grad_down = g_down.reshape(TP, rows, D).transpose(1, 0, 2)
    grads = [grad_in, grad_out, grad_gate, grad_down]

    def to_blocks(array):
        k, columns = array.shape[1:]
        shaped = array.reshape(rows, k, columns // B, B).transpose(1, 2, 0, 3)
        return shaped.reshape(k * (columns // B), rows, B)

    slots_here = left_stats.shape[0]
    total_slots = slots_here * devices
    owner = (block_slots[None, :] == jnp.arange(total_slots, dtype=jnp.int32)[:, None]).astype(BF)
    g_blocks = g_gate.reshape(TP, 2, rows, 2, UNITS).transpose(1, 3, 0, 2, 4).reshape(-1, rows, B)
    d_blocks = g_down.reshape(TP, rows, 2, B).transpose(0, 2, 1, 3).reshape(-1, rows, B)
    grad_blocks = jnp.concatenate([to_blocks(grad_in), to_blocks(grad_out), g_blocks, d_blocks], 0)
    product = lambda p, q: lax.dot_general(
        p, q, (((1,), (0,)), ((), ())), preferred_element_type=F32
    )
    returned, left_new, right_new = [], [], []
    for i in range(slots_here):
        send = jnp.einsum(
            "sb,bxy->sxy", owner[i::slots_here], grad_blocks, preferred_element_type=F32
        ).astype(BF)
        owned = exchange(send, ALL).reshape(B, B)
        direction = dot(dot(left_roots[i].astype(BF), owned, BF), right_inverse_roots[i].astype(BF))
        size = jnp.mean(direction * direction)
        direction = (direction * lax.rsqrt(size + STEP_EPS)).astype(BF)
        returned.append(exchange(direction.reshape(devices, rows, B), ALL))
        left_new.append(STAT_DECAY * left_stats[i] + (1.0 - STAT_DECAY) * dot_nt(owned, owned))
        right_new.append(STAT_DECAY * right_stats[i] + (1.0 - STAT_DECAY) * dot_tn(owned, owned))
    if slots_here == 1:
        returned = [returned[0][0::2], returned[0][1::2]]
    new_weights, offset = [], 0
    for w in weights:
        count = w.shape[1] * (w.shape[2] // B)
        here = slice(offset, offset + count)
        new_weights.append(update(w, block_slots[here], weight_size[here], *returned))
        offset += count
    return (
        layer_output,
        input_grad,
        *[g.astype(F32) for g in grads],
        gain_grads,
        *new_weights,
        norm_gains - GAIN_RATE * gain_grads,
        jnp.stack(left_new),
        jnp.stack(right_new),
    )


def solution(mesh):
    outer = mesh.shape["dp"] // TP
    fine = Mesh(mesh.devices.reshape(outer, 2, 2, 2, mesh.shape["seq"]), ALL)
    dp = ("o",) + TENSOR
    by_token = P(dp, "z", None)
    by_row = P(ALL, None, None)
    return jax.shard_map(
        on_device,
        mesh=fine,
        in_specs=(by_token,) * 2 + (by_row,) * 4 + (P(), P(dp), P()) + (by_row,) * 4,
        out_specs=(by_token,) * 2 + (by_row,) * 4 + (P(),) + (by_row,) * 4 + (P(),) + (by_row,) * 2,
        check_vma=False,
    )
```

time: 1570 us -> 1140 us (0.73)
  waiting for transfers between devices: 648 us -> 401 us
  blocking collectives: 173 us -> 0 us
  Pallas kernels: 0 us -> 112 us
  local copies, waits for them, and re-layouts: 236 us -> 159 us
  matrix products: 217 us -> 179 us
    ppermute x84 -> x62, waiting for transfers between devices: 347 us -> 169 us  [flip(): return lax.ppermute(value, axis, [(0, 1), (1, 0)])]
    pallas_call x0 -> x40, Pallas kernels: none -> 112 us  [the longest x4 24.5 us: assemble(): pl.pallas_call(kernel, in_specs=[pl.BlockSpec(memory_space=pl.ANY)] * len...]
    psum x1 -> x0, blocking collectives: 102 us -> none  [on_device(): sums = lax.psum(jnp.concatenate([gain_one, gain_two] + squares), ALL)]
    ppermute x0 -> x17, waiting for transfers between devices: none -> 81.3 us  [the longest x6 50.7 us: swap_z(): lax.ppermute(parts[i], 'z', [(j, j ^ i) for j in range(z_count)])]
    reduce_scatter x4 -> x3, waiting for transfers between devices: 77.5 us -> 0.01 us  [to_owners(): return lax.psum_scatter(grad, SHARD, scatter_dimension=0, tiled=True)]
    all_to_all x2 -> x0, blocking collectives: 71.1 us -> none  [exchange(): return lax.all_to_all(value, axes, split_axis=0, concat_axis=0, tiled=True)]
    all_gather x4 -> x3, waiting for transfers between devices: 58.6 us -> 15.3 us  [the longest x1 9.67 us: on_device(): every_gate = lax.all_gather(cut_gate, SHARD, axis=0, tiled=False)]
    unnamed x358 -> x243, local copies, waits for them, and re-layouts: 82.4 us -> 40.5 us
  transfers between devices with their start and end apart: 111 -> 104, of which waited for: 75 -> 47; matrix products, arithmetic and copies ran while one was open for 22% -> 36% of each run, Pallas kernels for 0% -> 6%
where the time goes in v2:
time: 1140 us; the launch traced here: 1130 us
  waiting for transfers between devices  401 us (35%)
  matrix products  179 us (16%)
  local copies, waits for them, and re-layouts  159 us (14%)
  starting transfers between devices  151 us (13%)
  Pallas kernels  112 us (10%)
  other arithmetic  108 us (9%)
  between operations  18.7 us (2%)
    ppermute x62, waiting for transfers between devices, flip(): return lax.ppermute(value, axis, [(0, 1), (1, 0)])  169 us
    all_to_all x15, waiting for transfers between devices, exchange(): return lax.all_to_all(value, axes, split_axis=0, concat_axis=0, tiled=True)  127 us
    all_to_all x15, starting transfers between devices, exchange(): return lax.all_to_all(value, axes, split_axis=0, concat_axis=0, tiled=True)  65.3 us
    dot_general x11, matrix products, dot_nt(): lax.dot_general(x, y, (((1,), (1,)), ((), ())), preferred_element_type=F32)  59.8 us
    dot_general x11, matrix products, dot(): lax.dot_general(x, y, (((1,), (0,)), ((), ())), preferred_element_type=F32)  59.2 us
    dot_general x6, matrix products, dot_tn(): lax.dot_general(x, y, (((0,), (0,)), ((), ())), preferred_element_type=F32)  54 us
    ppermute x6, waiting for transfers between devices, swap_z(): lax.ppermute(parts[i], 'z', [(j, j ^ i) for j in range(z_count)])  50.7 us
    ppermute x62, starting transfers between devices, flip(): return lax.ppermute(value, axis, [(0, 1), (1, 0)])  47 us
  transfers between devices with their start and end apart: 104, of which 47 were waited for; matrix products, arithmetic and copies ran while one was open for 36% of the time, Pallas kernels for 6%

profile of v2, /device:TPU:0, one launch (start us, length us, event | category | flops | bytes accessed | tf_op | source)
XLA Modules:
  0.0 1129.0 jit_solution(1175262476518896749)
XLA Ops:
  73.5 27.1 %collective-permute-done.3 = bf16[64,2048]{1,0:T(8,128)(2,1)S(1)} collective-permute-done((bf16[64,2048]{1,0:T(8,128)(2,1)S(1)}, bf16[64,2048]{1,0:T(8,128)(2,1)S(1)}, u32[]{:S(2)}, u32[]{:S(2)}) %collective-permute-start.3) | collective-permute-done | bytes 262176 | tf_op jit(solution)/shard_map/ppermute | solution.py:178
  107.7 22.7 %collective-permute-done.5.refs_1_ = bf16[256,2048]{1,0:T(8,128)(2,1)S(1)} collective-permute-done((bf16[256,2048]{1,0:T(8,128)(2,1)S(1)}, bf16[256,2048]{1,0:T(8,128)(2,1)S(1)}, u32[]{:S(2)}, u32[]{:S(2)}) %collective-permute-start.5) | collective-permute-done | bytes 1048608 | tf_op jit(solution)/shard_map/ppermute | solution.py:51
  213.6 9.7 attend.1
  247.4 21.2 %collective-permute-done.23 = bf16[64,2048]{1,0:T(8,128)(2,1)S(1)} collective-permute-done((bf16[64,2048]{1,0:T(8,128)(2,1)S(1)}, bf16[64,2048]{1,0:T(8,128)(2,1)S(1)}, u32[]{:S(2)}, u32[]{:S(2)}) %collective-permute-start.23) | collective-permute-done | bytes 262176 | tf_op jit(solution)/shard_map/ppermute | solution.py:178
  280.2 16.4 %collective-permute-done.19 = bf16[256,2048]{1,0:T(8,128)(2,1)S(1)} collective-permute-done((bf16[256,2048]{1,0:T(8,128)(2,1)S(1)}, bf16[256,2048]{1,0:T(8,128)(2,1)S(1)}, u32[]{:S(2)}, u32[]{:S(2)}) %collective-permute-start.19) | collective-permute-done | bytes 1048608 | tf_op jit(solution)/shard_map/ppermute | solution.py:51
  318.4 9.7 all-gather.9.cloned.1.call-done
  329.2 9.7 collective-permute-done.21.refs_1_
  344.7 11.5 %collective-permute-done.26.refs_3_ = bf16[128,2048]{1,0:T(8,128)(2,1)S(1)} collective-permute-done((bf16[128,2048]{1,0:T(8,128)(2,1)}, bf16[128,2048]{1,0:T(8,128)(2,1)S(1)}, u32[]{:S(2)}, u32[]{:S(2)}) %collective-permute-start.26) | collective-permute-done | bytes 524320 | tf_op jit(solution)/shard_map/ppermute | solution.py:51
  373.7 24.5 %gate_forward.1 = (bf16[2048,1024]{1,0:T(8,128)(2,1)S(1)}, f32[2048,1024]{1,0:T(8,128)}, f32[2048,1024]{1,0:T(8,128)}) custom-call(bf16[2048,2048]{1,0:T(8,128)(2,1)} %assemble.5.rows.refs_1_, bf16[2048,2048]{1,0:T(8,128)(2,1)} %bitcast.357), custom_call_target="tpu_custom_call" | custom-call | flops 17179869184 | bytes 37748736 | tf_op jit(solution)/shard_map/gate_forward/pallas_call | solution.py:316
  404.6 11.1 collective-permute-done.35.refs_3_
  425.4 11.4 %convolution_convert_fusion.1 = bf16[1024,2048]{1,0:T(8,128)(2,1)S(1)} fusion(bf16[2048,1024]{1,0:T(8,128)(2,1)S(1)} %copy-done.1, bf16[2048,2048]{1,0:T(8,128)(2,1)} %assemble.6.refs_0_), kind=kOutput, calls=%fused_computation.36 | convolution fusion | flops 8592031744 | bytes 16777216 | tf_op jit(solution)/shard_map/dot_general | solution.py:47
  442.3 18.2 %gate_back.1 = bf16[2048,2048]{1,0:T(8,128)(2,1)} custom-call(bf16[2048,2048]{1,0:T(8,128)(2,1)} %after.42.rows, bf16[1024,2048]{1,0:T(8,128)(2,1)S(1)} %bitcast.309, f32[2048,1024]{1,0:T(8,128)} %get-tuple-element.24.gate_slope, f32[2048,1024]{1,0:T(8,128)} %get-tuple-element.25.up_slope), custom_call_target="tpu_custom_call" | custom-call | flops 8589934592 | bytes 37748736 | tf_op jit(solution)/shard_map/gate_back/pallas_call | solution.py:341
  468.4 10.0 convolution_convert_fusion.10
  501.6 22.2 %convolution_convert_fusion.refs_1_ = bf16[2048,2048]{1,0:T(8,128)(2,1)} fusion(bf16[2048,2048]{1,0:T(8,128)(2,1)S(1)} %bitcast.330, bf16[2048,2048]{1,0:T(8,128)(2,1)} %gate_back.1), kind=kOutput, calls=%fused_computation.2 | convolution fusion | flops 17184063488 | bytes 25165824 | tf_op jit(solution)/shard_map/dot_general | solution.py:47
  562.7 21.9 %collective-permute-done.48.refs_1_ = bf16[256,2048]{1,0:T(8,128)(2,1)S(1)} collective-permute-done((bf16[256,2048]{1,0:T(8,128)(2,1)S(1)}, bf16[256,2048]{1,0:T(8,128)(2,1)S(1)}, u32[]{:S(2)}, u32[]{:S(2)}) %collective-permute-start.48) | collective-permute-done | bytes 1048608 | tf_op jit(solution)/shard_map/ppermute | solution.py:51
  602.9 10.5 all-to-all-done.8.refs_2_
  643.6 12.2 %attend_back.1 = (f32[2,1024,256]{2,1,0:T(8,128)}, f32[2,1024,256]{2,1,0:T(8,128)}, f32[2,1024,256]{2,1,0:T(8,128)}) custom-call(s32[2,1024,1]{2,1,0:T(8,128)S(1)} %copy-done.22, s32[2,1,1024]{2,1,0:T(1,128)S(1)} %copy-done.26, bf16[2,1024,256]{2,1,0:T(8,128)(2,1)S(1)} %copy-done.24, bf16[2,1024,256]{2,1,0:T(8,128)(2,1)S(1)} %copy-done.20, ...), custom_call_target="tpu_custom_call" | custom-call | flops 5368709120 | bytes 10485760 | tf_op jit(solution)/shard_map/attend_back/pallas_call | solution.py:286
  761.9 9.1 collective-permute-done.68
  879.0 42.1 %all-to-all-done.11 = bf16[32,32,1024]{2,1,0:T(8,128)(2,1)} async-done(((bf16[32,32,1024]{2,1,0:T(8,128)(2,1)}), bf16[32,32,1024]{2,1,0:T(8,128)(2,1)}, u32[]{:S(2)}, u32[]{:S(2)}) %all-to-all-start.11) | async-done | bytes 2097184 | tf_op jit(solution)/shard_map/all_to_all | solution.py:164
  979.9 10.2 multiply_reduce_fusion.1
  1006.8 10.2 multiply_reduce_fusion
  1035.9 9.3 all-to-all-done.12.refs_0_.refs_2_.refs_4_.refs_6_.refs_8_.refs_10_.refs_12_.refs_14_
  1065.8 31.0 %all-to-all-done.14.refs_1_.refs_3_.refs_5_.refs_7_.refs_9_.refs_11_.refs_13_.refs_15_ = bf16[32,32,1024]{2,1,0:T(8,128)(2,1)} async-done(((bf16[32,32,1024]{2,1,0:T(8,128)(2,1)}), bf16[32,32,1024]{2,1,0:T(8,128)(2,1)}, u32[]{:S(2)}, u32[]{:S(2)}) %all-to-all-start.14) | async-done | bytes 2097184 | tf_op jit(solution)/shard_map/all_to_all | solution.py:164
  1104.6 11.9 %update.6 = f32[32,2,16384]{2,1,0:T(2,128)} custom-call(s32[32]{0:T(128)S(1)} %slice.563.slots, f32[32]{0:T(128)S(1)} %slice.564.sizes, f32[32,2,16384]{2,1,0:T(2,128)} %weight.6, bf16[32,32,1024]{2,1,0:T(8,128)(2,1)S(1)} %all-to-all-done.12.refs_0_.refs_2_.refs_4_.refs_6_.refs_8_.refs_10_.refs_12_.refs_14_, ...), custom_call_target="tpu_custom_call" | custom-call | tf_op jit(solution)/shard_map/update/pallas_call | solution.py:375
  (708 shorter events, 716.8 us)
Async XLA Ops:
  37.0 101.3 %all-gather.7.cloned.1.call-start = ((), (), s32[]{:S(2)}) async-start(), calls=%async_computation.21 | async-start | bytes 3932160 | tf_op jit(solution)/shard_map/all_gather | solution.py:449
  67.2 75.6 %all-to-all-start.3 = ((bf16[8,2,32,2048]{3,2,1,0:T(8,128)(2,1)}), bf16[8,2,32,2048]{3,2,1,0:T(8,128)(2,1)}, u32[]{:S(2)}, u32[]{:S(2)}) async-start(bf16[8,2,32,2048]{3,2,1,0:T(8,128)(2,1)} %after.30), calls=%async_computation.3 | async-start | bytes 4194304 | tf_op jit(solution)/shard_map/all_to_all | solution.py:164
  107.7 50.4 %collective-permute-start.8 = (bf16[256,2048]{1,0:T(8,128)(2,1)S(1)}, bf16[256,2048]{1,0:T(8,128)(2,1)}, u32[]{:S(2)}, u32[]{:S(2)}) collective-permute-start(bf16[256,2048]{1,0:T(8,128)(2,1)S(1)} %fusion.10.refs_0_), channel_id=1, source_target_pairs={{0,4},{4,0},{1,5},{5,1},{2,6},{6,2},{3,7},{7,3},{8,12},{12,8},{9,1... | collective-permute-start | bytes 3145736 | tf_op jit(solution)/shard_map/ppermute | solution.py:51
  147.2 180.9 %all-gather.9.cloned.1.call-start = ((), (), s32[]{:S(2)}) async-start(), calls=%async_computation.22 | async-start | bytes 10485760 | tf_op jit(solution)/shard_map/all_gather | solution.py:461
  227.2 212.1 %all-gather.11.cloned.1.call-start = ((), (), s32[]{:S(2)}) async-start(), calls=%async_computation.23 | async-start | bytes 5242880 | tf_op jit(solution)/shard_map/all_gather | solution.py:494
  230.2 38.4 %collective-permute-start.18 = (bf16[512,2048]{1,0:T(8,128)(2,1)}, bf16[512,2048]{1,0:T(8,128)(2,1)}, u32[]{:S(2)}, u32[]{:S(2)}) collective-permute-start(bf16[512,2048]{1,0:T(8,128)(2,1)} %convolution_convert_fusion.4), channel_id=1, source_target_pairs={{0,4},{4,0},{1,5},{5,1},{2,6},{6,2},{3,7},{7,3},{8,12},{12,8},{9,1... | collective-permute-start | bytes 6291464 | tf_op jit(solution)/shard_map/ppermute | solution.py:51
  233.6 39.4 %collective-permute-start.15 = (bf16[512,2048]{1,0:T(8,128)(2,1)}, bf16[512,2048]{1,0:T(8,128)(2,1)}, u32[]{:S(2)}, u32[]{:S(2)}) collective-permute-start(bf16[512,2048]{1,0:T(8,128)(2,1)} %convolution_convert_fusion.5), channel_id=1, source_target_pairs={{0,4},{4,0},{1,5},{5,1},{2,6},{6,2},{3,7},{7,3},{8,12},{12,8},{9,1... | collective-permute-start | bytes 6291464 | tf_op jit(solution)/shard_map/ppermute | solution.py:51
  328.1 258.7 %reduce-scatter.4.cloned.1.call-start = ((), (), s32[]{:S(2)}) async-start(), calls=%async_computation.18 | async-start | bytes 5242880 | tf_op jit(solution)/shard_map/reduce_scatter | solution.py:509
  329.1 36.7 %collective-permute-start.27 = (bf16[256,2048]{1,0:T(8,128)(2,1)S(1)}, bf16[256,2048]{1,0:T(8,128)(2,1)}, u32[]{:S(2)}, u32[]{:S(2)}) collective-permute-start(bf16[256,2048]{1,0:T(8,128)(2,1)S(1)} %multiply_convert_fusion.2.refs_0_), channel_id=1, source_target_pairs={{0,4},{4,0},{1,5},{5,1},{2,6},{6,2},{3,7},{7,3},{8,12},{12,8},{9,1... | collective-permute-start | bytes 3145736 | tf_op jit(solution)/shard_map/ppermute | solution.py:51
  373.7 44.2 %collective-permute-start.36 = (bf16[256,2048]{1,0:T(8,128)(2,1)}, bf16[256,2048]{1,0:T(8,128)(2,1)}, u32[]{:S(2)}, u32[]{:S(2)}) collective-permute-start(bf16[256,2048]{1,0:T(8,128)(2,1)} %after.39.refs_0_), channel_id=1, source_target_pairs={{0,4},{4,0},{1,5},{5,1},{2,6},{6,2},{3,7},{7,3},{8,12},{12,8},{9,1... | collective-permute-start | bytes 3145736 | tf_op jit(solution)/shard_map/ppermute | solution.py:51
  468.0 252.6 %reduce-scatter.6.cloned.1.call-start = ((), (), s32[]{:S(2)}) async-start(), calls=%async_computation.19 | async-start | bytes 10485760 | tf_op jit(solution)/shard_map/reduce_scatter | solution.py:509
  488.8 43.4 %collective-permute-start.46 = (bf16[256,2048]{1,0:T(8,128)(2,1)S(1)}, bf16[256,2048]{1,0:T(8,128)(2,1)S(1)}, u32[]{:S(2)}, u32[]{:S(2)}) collective-permute-start(bf16[256,2048]{1,0:T(8,128)(2,1)S(1)} %slice.819), channel_id=1, source_target_pairs={{0,8},{8,0},{1,9},{9,1},{2,10},{10,2},{3,11},{11,3},{4,12},{12,4},... | collective-permute-start | bytes 3145736 | tf_op jit(solution)/shard_map/ppermute | solution.py:51
  500.9 36.6 %collective-permute-start.43 = (bf16[256,2048]{1,0:T(8,128)(2,1)}, bf16[256,2048]{1,0:T(8,128)(2,1)}, u32[]{:S(2)}, u32[]{:S(2)}) collective-permute-start(bf16[256,2048]{1,0:T(8,128)(2,1)} %slice.820), channel_id=1, source_target_pairs={{0,16},{16,0},{1,17},{17,1},{2,18},{18,2},{3,19},{19,3},{4,20},{20... | collective-permute-start | bytes 3145736 | tf_op jit(solution)/shard_map/ppermute | solution.py:51
  562.7 58.8 %collective-permute-start.51 = (bf16[256,2048]{1,0:T(8,128)(2,1)S(1)}, bf16[256,2048]{1,0:T(8,128)(2,1)}, u32[]{:S(2)}, u32[]{:S(2)}) collective-permute-start(bf16[256,2048]{1,0:T(8,128)(2,1)S(1)} %get-tuple-element.104.refs_0_), channel_id=1, source_target_pairs={{0,4},{4,0},{1,5},{5,1},{2,6},{6,2},{3,7},{7,3},{8,12},{12,8},{9,1... | collective-permute-start | bytes 3145736 | tf_op jit(solution)/shard_map/ppermute | solution.py:51
  593.0 214.1 %reduce-scatter.8.cloned.1.call-start = ((), (), s32[]{:S(2)}) async-start(), calls=%async_computation.20 | async-start | bytes 3932160 | tf_op jit(solution)/shard_map/reduce_scatter | solution.py:509
  726.5 53.9 %collective-permute-start.64 = (bf16[64,2048]{1,0:T(8,128)(2,1)}, bf16[64,2048]{1,0:T(8,128)(2,1)}, u32[]{:S(2)}, u32[]{:S(2)}) collective-permute-start(bf16[64,2048]{1,0:T(8,128)(2,1)} %bitcast.60), channel_id=1, source_target_pairs={{0,2},{1,3},{2,0},{3,1},{4,6},{5,7},{6,4},{7,5},{8,10},{9,11},{10,... | collective-permute-start | bytes 786440 | tf_op jit(solution)/shard_map/ppermute | solution.py:200
  727.0 54.3 %collective-permute-start.65 = (bf16[64,2048]{1,0:T(8,128)(2,1)}, bf16[64,2048]{1,0:T(8,128)(2,1)S(1)}, u32[]{:S(2)}, u32[]{:S(2)}) collective-permute-start(bf16[64,2048]{1,0:T(8,128)(2,1)} %bitcast.62), channel_id=1, source_target_pairs={{0,3},{1,2},{2,1},{3,0},{4,7},{5,6},{6,5},{7,4},{8,11},{9,10},{10,... | collective-permute-start | bytes 786440 | tf_op jit(solution)/shard_map/ppermute | solution.py:200
  748.1 39.7 %all-to-all-start.7 = ((bf16[8,2,32,2048]{3,2,1,0:T(8,128)(2,1)}), bf16[8,2,32,2048]{3,2,1,0:T(8,128)(2,1)S(1)}, u32[]{:S(2)}, u32[]{:S(2)}) async-start(bf16[8,2,32,2048]{3,2,1,0:T(8,128)(2,1)} %bitcast.368), calls=%async_computation.9 | async-start | bytes 4194304 | tf_op jit(solution)/shard_map/all_to_all | solution.py:164
  761.2 38.3 %collective-permute-start.72 = (bf16[128,2048]{1,0:T(8,128)(2,1)}, bf16[128,2048]{1,0:T(8,128)(2,1)}, u32[]{:S(2)}, u32[]{:S(2)}) collective-permute-start(bf16[128,2048]{1,0:T(8,128)(2,1)} %slice.823), channel_id=1, source_target_pairs={{0,16},{16,0},{1,17},{17,1},{2,18},{18,2},{3,19},{19,3},{4,20},{20... | collective-permute-start | bytes 1572872 | tf_op jit(solution)/shard_map/ppermute | solution.py:51
  787.8 46.4 %all-to-all-start.6 = ((bf16[8,1,32,2048]{3,2,1,0:T(8,128)(2,1)}), bf16[8,1,32,2048]{3,2,1,0:T(8,128)(2,1)S(1)}, u32[]{:S(2)}, u32[]{:S(2)}) async-start(bf16[8,1,32,2048]{3,2,1,0:T(8,128)(2,1)} %bitcast.379), calls=%async_computation.7 | async-start | bytes 2097152 | tf_op jit(solution)/shard_map/all_to_all | solution.py:164
  869.7 51.3 %all-to-all-start.11 = ((bf16[32,32,1024]{2,1,0:T(8,128)(2,1)}), bf16[32,32,1024]{2,1,0:T(8,128)(2,1)}, u32[]{:S(2)}, u32[]{:S(2)}) async-start(bf16[32,32,1024]{2,1,0:T(8,128)(2,1)} %copy.268), calls=%async_computation.14 | async-start | bytes 4194304 | tf_op jit(solution)/shard_map/all_to_all | solution.py:164
  921.1 73.7 %all-to-all-start.13 = ((bf16[32,32,1024]{2,1,0:T(8,128)(2,1)}), bf16[32,32,1024]{2,1,0:T(8,128)(2,1)}, u32[]{:S(2)}, u32[]{:S(2)}) async-start(bf16[32,32,1024]{2,1,0:T(8,128)(2,1)} %copy.269), calls=%async_computation.16 | async-start | bytes 4194304 | tf_op jit(solution)/shard_map/all_to_all | solution.py:164
  994.8 50.4 %all-to-all-start.12 = ((bf16[32,32,1024]{2,1,0:T(8,128)(2,1)}), bf16[32,32,1024]{2,1,0:T(8,128)(2,1)S(1)}, u32[]{:S(2)}, u32[]{:S(2)}) async-start(bf16[32,32,1024]{2,1,0:T(8,128)(2,1)} %bitcast.354), calls=%async_computation.15 | async-start | bytes 4194304 | tf_op jit(solution)/shard_map/all_to_all | solution.py:164
  1045.2 51.6 %all-to-all-start.14 = ((bf16[32,32,1024]{2,1,0:T(8,128)(2,1)}), bf16[32,32,1024]{2,1,0:T(8,128)(2,1)}, u32[]{:S(2)}, u32[]{:S(2)}) async-start(bf16[32,32,1024]{2,1,0:T(8,128)(2,1)} %bitcast.356), calls=%async_computation.17 | async-start | bytes 4194304 | tf_op jit(solution)/shard_map/all_to_all | solution.py:164
  (189 other events, 3021.7 us)
Sparse Core Ops, SparseCore 0:
  64.5 73.7 all-gather.6
  149.6 178.4 all-gather.8
  330.2 78.8 all-gather.10
  468.1 75.3 reduce-scatter.3
  545.8 144.9 reduce-scatter.5
  720.7 77.3 reduce-scatter.7

commit v3 on v2

--- a/solution.py
+++ b/solution.py
@@ -124,20 +124,25 @@
     )
 
 
-def scatter_tokens(rows, times, middle=(), end=()):
+def core_sums(rows, times):
     quarter = rows.shape[0] // 4
     p_far = flip(times(rows[quarter : 2 * quarter]).astype(BF), "c")
     q_far = flip(times(rows[3 * quarter :]).astype(BF), "c")
     p = times(rows[:quarter]) + p_far.astype(F32)
     q = times(rows[2 * quarter : 3 * quarter]) + q_far.astype(F32)
-    e = quarter // 2
-    p_got = flip(p[e:].astype(BF), "a")
-    q_got = flip(q[e:].astype(BF), "b")
+    return p, q
+
+
+def chip_sums(p, q, start=(), middle=(), end=()):
+    e, f = p.shape[0] // 2, p.shape[0] // 4
+    p_give, q_give = p[e:].astype(BF), q[e:].astype(BF)
+    if start:
+        p_give, q_give = after(p_give, *start), after(q_give, *start)
+    p_got, q_got = flip(p_give, "a"), flip(q_give, "b")
     if middle:
         p_got, q_got = after(p_got, *middle), after(q_got, *middle)
     p_sum = p[:e] + p_got.astype(F32)
     q_sum = q[:e] + q_got.astype(F32)
-    f = e // 2
     p_got = flip(p_sum[f:].astype(BF), "b")
     q_got = flip(q_sum[f:].astype(BF), "a")
     if end:
@@ -145,8 +150,8 @@
     return jnp.concatenate([p_sum[:f] + p_got.astype(F32), q_sum[:f] + q_got.astype(F32)], 0)
 
 
-def sum_everywhere(value):
-    for axis in ALL:
+def sum_over(value, axes):
+    for axis in axes:
         count = lax.axis_size(axis)
         bit = 1
         while bit < count:
@@ -155,6 +160,30 @@
     return value
 
 
+def gather_shards(value):
+    parts = [value]
+    for axis in SHARD:
+        count = lax.axis_size(axis)
+        if count > 1:
+            parts = [
+                part if i == 0 else lax.ppermute(part, axis, [(j, j ^ i) for j in range(count)])
+                for part in parts
+                for i in range(count)
+            ]
+    return parts
+
+
+def sum_shards(parts):
+    own = lax.axis_index(SHARD)
+    stacked = jnp.zeros((len(parts), *parts[0].shape), parts[0].dtype)
+    for i, part in enumerate(parts):
+        stacked = lax.dynamic_update_index_in_dim(stacked, part, own ^ i, 0)
+    total = stacked[0]
+    for i in range(1, len(parts)):
+        total = total + stacked[i]
+    return total
+
+
 def swap_halves(value):
     half = value.shape[1] // 2
     return jnp.concatenate([value[:, half:], value[:, :half]], 1)
@@ -171,36 +200,37 @@
     return parts.reshape(TP * seqs, n, width)
 
 
-def swap_z(value, z_count):
+def swap_z(value):
+    z, count = lax.axis_index("z"), value.shape[0]
+    parts = [lax.dynamic_index_in_dim(value, z ^ i, 0, keepdims=False) for i in range(count)]
+    return parts[:1] + [
+        lax.ppermute(parts[i], "z", [(j, j ^ i) for j in range(count)]) for i in range(1, count)
+    ]
+
+
+def by_sequence(parts, m):
+    n = parts[0].shape[0] // m
+    return jnp.concatenate([part[s * n : (s + 1) * n] for s in range(m) for part in parts], 0)
+
+
+def to_z(values, m, z_count):
+    n = values.shape[0] // (m * z_count)
+    parts = values.reshape(m, z_count, n, D).transpose(1, 0, 2, 3).reshape(z_count, m * n, D)
     z = lax.axis_index("z")
-    parts = [lax.dynamic_index_in_dim(value, z ^ i, 0, keepdims=False) for i in range(z_count)]
     return [
-        parts[i] if i == 0 else lax.ppermute(parts[i], "z", [(j, j ^ i) for j in range(z_count)])
+        parts[i]
+        if i == 0
+        else lax.ppermute(parts[i], "z", [(j, j ^ i) for j in range(z_count)])
         for i in range(z_count)
     ]
 
 
-def reshard(parts, z_count):
-    every, n, width = parts.shape
-    m = every // z_count
-    parts = swap_z(parts.reshape(z_count, m * n, width), z_count)
-    return jnp.concatenate([part[s * n : (s + 1) * n] for s in range(m) for part in parts], 0)
-
-
-def reshard_back(values, z_count, seqs):
-    m = TP * seqs // z_count
-    n = values.shape[0] // (m * z_count)
-    width = values.shape[1]
+def in_z_order(parts):
     z = lax.axis_index("z")
-    parts = values.reshape(m, z_count, n, width).transpose(1, 0, 2, 3).reshape(z_count, m * n, width)
-    out = jnp.zeros_like(parts)
-    for i in range(z_count):
-        part = parts[i]
-        if i > 0:
-            part = lax.ppermute(part, "z", [(j, j ^ i) for j in range(z_count)])
+    out = jnp.zeros((len(parts), *parts[0].shape), parts[0].dtype)
+    for i, part in enumerate(parts):
         out = lax.dynamic_update_index_in_dim(out, part, z ^ i, 0)
-    parts = exchange(out.reshape(TP, seqs, n, width), TENSOR)
-    return parts.transpose(1, 0, 2, 3).reshape(seqs, TP * n, width)
+    return out
 
 
 def rms_scale(value):
@@ -232,12 +262,12 @@
 
 
 def attend_back_kernel(
-    limit, place, query, key, value, log_total, out_grad, query_grad, key_grad, value_grad
+    core, limit, place, query, key, value, log_total, out_grad, cosine, sine, query_grad, keep, give
 ):
     @pl.when(pl.program_id(1) == 0)
     def _():
-        key_grad[...] = jnp.zeros_like(key_grad)
-        value_grad[...] = jnp.zeros_like(value_grad)
+        keep[...] = jnp.zeros_like(keep)
+        give[...] = jnp.zeros_like(give)
 
     scores = dot_nt(query[0], key[0]) * HEAD ** (-0.5)
     scores = jnp.where(place[0] <= limit[0], scores, MASKED)
@@ -245,9 +275,12 @@
     share_grad = dot_nt(out_grad[0], value[0])
     inner = jnp.sum(shares * share_grad, -1, keepdims=True)
     score_grad = (shares * (share_grad - inner)).astype(BF)
-    query_grad[0] = dot(score_grad, key[0]) * HEAD ** (-0.5)
-    key_grad[0] += dot_tn(score_grad, query[0]) * HEAD ** (-0.5)
-    value_grad[0] += dot_tn(shares.astype(BF), out_grad[0])
+    turned = dot(score_grad, key[0]) * HEAD ** (-0.5)
+    query_grad[0] = rotate(turned, cosine[0], -sine[0]).astype(BF)
+    key_grad = dot_tn(score_grad, query[0]) * HEAD ** (-0.5)
+    value_grad = dot_tn(shares.astype(BF), out_grad[0])
+    keep[0] += jnp.where(core[0] == 0, key_grad, value_grad)
+    give[0] += jnp.where(core[0] == 0, value_grad, key_grad)
 
 
 def attention_specs(length, block):
@@ -279,7 +312,7 @@
     )(limit, place, query, key, value)
 
 
-def attend_back(limit, place, query, key, value, log_total, out_grad):
+def attend_back(core, limit, place, query, key, value, log_total, out_grad, cosine, sine):
     m, length = query.shape[:2]
     block = min(256, length)
     by_query, whole, row = attention_specs(length, block)
@@ -287,10 +320,12 @@
         attend_back_kernel,
         grid=(m, length // block),
         in_specs=[
+            pl.BlockSpec(memory_space=pltpu.SMEM),
             by_query(1), row, by_query(HEAD), whole(HEAD), whole(HEAD), by_query(1), by_query(HEAD),
+            by_query(HEAD // 2), by_query(HEAD // 2),
         ],
         out_specs=[by_query(HEAD), whole(HEAD), whole(HEAD)],
-        out_shape=[jax.ShapeDtypeStruct((m, length, HEAD), F32)] * 3,
+        out_shape=[jax.ShapeDtypeStruct((m, length, HEAD), t) for t in (BF, F32, F32)],
         compiler_params=pltpu.CompilerParams(vmem_limit_bytes=VMEM_BYTES),
         cost_estimate=pl.CostEstimate(
             flops=10 * m * length * length * HEAD,
@@ -298,7 +333,140 @@
             transcendentals=m * length * length,
         ),
         name="attend_back",
-    )(limit, place, query, key, value, log_total, out_grad)
+    )(core, limit, place, query, key, value, log_total, out_grad, cosine, sine)
+
+
+def mix_kernel(rows, weight, cosine, sine, own_cosine, own_sine, query, own):
+    mixed = dot(rows[...], weight[...])
+    query[...] = rotate(mixed[:, :HEAD], cosine[...], sine[...]).astype(BF)
+    own[...] = rotate(mixed[:, HEAD:], own_cosine[...], own_sine[...]).astype(BF)
+
+
+def mix_forward(rows, weight, *tables):
+    count, block = rows.shape[0], 256
+    by_row = lambda width: pl.BlockSpec((block, width), lambda i: (i, 0))
+    return pl.pallas_call(
+        mix_kernel,
+        grid=(count // block,),
+        in_specs=[by_row(D), pl.BlockSpec((D, 2 * HEAD), lambda i: (0, 0))]
+        + [by_row(HEAD // 2)] * 4,
+        out_specs=[by_row(HEAD)] * 2,
+        out_shape=[jax.ShapeDtypeStruct((count, HEAD), BF)] * 2,
+        compiler_params=pltpu.CompilerParams(vmem_limit_bytes=VMEM_BYTES),
+        cost_estimate=pl.CostEstimate(
+            flops=4 * count * D * HEAD,
+            bytes_accessed=2 * (count * D + 2 * D * HEAD) + 8 * count * HEAD,
+            transcendentals=0,
+        ),
+        name="mix_forward",
+    )(rows, weight, *tables)
+
+
+def mix_back_kernel(query_grad, keep, got, cosine, sine, out):
+    out[0, :, :HEAD] = query_grad[0]
+    out[0, :, HEAD:] = rotate(keep[0] + got[0], cosine[0], -sine[0]).astype(BF)
+
+
+def mix_back(query_grad, keep, got, cosine, sine):
+    m, length = keep.shape[:2]
+    block = min(256, length // 2)
+    blocks = length // block
+    spec = lambda width: pl.BlockSpec((1, block, width), lambda s, i: (s, i, 0))
+    swapped = pl.BlockSpec((1, block, HEAD), lambda s, i: (s, (i + blocks // 2) % blocks, 0))
+    return pl.pallas_call(
+        mix_back_kernel,
+        grid=(m, blocks),
+        in_specs=[spec(HEAD), spec(HEAD), swapped, spec(HEAD // 2), spec(HEAD // 2)],
+        out_specs=spec(2 * HEAD),
+        out_shape=jax.ShapeDtypeStruct((m, length, 2 * HEAD), BF),
+        compiler_params=pltpu.CompilerParams(vmem_limit_bytes=VMEM_BYTES),
+        name="mix_back",
+    )(query_grad, keep, got, cosine, sine)
+
+
+def cut_gate_kernel(other, gate, up, out):
+    for k in range(2):
+        out[0, k, :, :UNITS] = gate[:, k, :].astype(BF)
+        out[0, k, :, UNITS:] = up[:, k, :].astype(BF)
+
+
+def cut_gate_up(weight, other):
+    rows = weight.shape[0]
+    return pl.pallas_call(
+        cut_gate_kernel,
+        grid=(TP,),
+        in_specs=[
+            pl.BlockSpec(memory_space=pl.ANY),
+            pl.BlockSpec((rows, 2, UNITS), lambda j: (0, 0, j)),
+            pl.BlockSpec((rows, 2, UNITS), lambda j: (0, 0, TP + j)),
+        ],
+        out_specs=pl.BlockSpec((1, 2, rows, 2 * UNITS), lambda j: (j, 0, 0, 0)),
+        out_shape=jax.ShapeDtypeStruct((TP, 2, rows, 2 * UNITS), BF),
+        compiler_params=pltpu.CompilerParams(vmem_limit_bytes=VMEM_BYTES),
+        name="cut_gate_up",
+    )(other, weight, weight)
+
+
+def weight_grad_kernel(left, right, *refs):
+    out = refs[-1]
+    _, z, holders, _, rows, columns = out.shape
+    product = dot_tn(left[...], right[...], BF).reshape(holders, z, rows, columns)
+    for h in range(holders):
+        for i in range(z):
+            out[0, i, h, 0] = product[h, i]
+
+
+def weight_grad(left, right, outer, z_count, rows, others=()):
+    count, features = left.shape
+    lead, columns = features // B, right.shape[1]
+    tile = 256
+    holders = tile // (z_count * rows)
+    per_outer, per_lead = TP // holders, B // tile
+    return pl.pallas_call(
+        weight_grad_kernel,
+        grid=(features // tile,),
+        in_specs=[
+            pl.BlockSpec((count, tile), lambda i: (0, i)),
+            pl.BlockSpec((count, columns), lambda i: (0, 0)),
+        ]
+        + [pl.BlockSpec(memory_space=pl.ANY)] * len(others),
+        out_specs=pl.BlockSpec(
+            (1, z_count, holders, 1, rows, columns),
+            lambda i: (i % per_lead // per_outer, 0, i % per_outer, i // per_lead, 0, 0),
+        ),
+        out_shape=jax.ShapeDtypeStruct((outer, z_count, TP, lead, rows, columns), BF),
+        compiler_params=pltpu.CompilerParams(vmem_limit_bytes=VMEM_BYTES),
+        cost_estimate=pl.CostEstimate(
+            flops=2 * count * features * columns,
+            bytes_accessed=2 * (count * (features + columns) + features * columns),
+            transcendentals=0,
+        ),
+        name="weight_grad",
+    )(left, right, *others)
+
+
+def direction_kernel(left, right, grad, out):
+    half = dot(left[0].astype(BF), grad[...], BF)
+    full = dot(half, right[0].astype(BF))
+    size = jnp.sum(full * full) / (B * B)
+    out[...] = (full * lax.rsqrt(size + STEP_EPS)).astype(BF)
+
+
+def unit_direction(index, left, right, grad):
+    one = pl.BlockSpec((1, B, B), lambda i: (index, 0, 0))
+    whole = pl.BlockSpec((B, B), lambda i: (0, 0))
+    return pl.pallas_call(
+        direction_kernel,
+        grid=(1,),
+        in_specs=[one, one, whole],
+        out_specs=whole,
+        out_shape=jax.ShapeDtypeStruct((B, B), BF),
+        compiler_params=pltpu.CompilerParams(vmem_limit_bytes=VMEM_BYTES),
+        cost_estimate=pl.CostEstimate(
+            flops=4 * B**3, bytes_accessed=12 * B * B, transcendentals=0
+        ),
+        name="unit_direction",
+    )(left, right, grad)
 
 
 def gate_kernel(rows, weight, hidden, gate_slope, up_slope):
@@ -424,7 +592,8 @@
     heads = low_in[:, :, :QD].reshape(rows, 2, HEADS, HEAD)
     keys_values = low_in[:, :, QD:].reshape(rows, 2, 2, KV_HEADS, HEAD).transpose(0, 1, 3, 2, 4)
     mixed_cols = jnp.concatenate([heads, keys_values.reshape(rows, 2, HEADS, HEAD)], -1)
-    mixed_cols = exchange(mixed_cols.transpose(2, 1, 0, 3), TENSOR)
+    x_parts = exchange(share_tokens(tokens), TENSOR)
+    mixed_cols = exchange(after(mixed_cols.transpose(2, 1, 0, 3), x_parts), TENSOR)
 
     low_out = attend_out.astype(BF).transpose(1, 0, 2)
     holders = range(outer * TP)
@@ -452,15 +621,6 @@
     w_out = joined[:, mix_rows:].reshape(outer, z_count, 4, 2, rows, D // 4)
     w_out = w_out.transpose(0, 3, 1, 4, 2, 5).reshape(HEAD, D)
 
-    x_parts = exchange(after(share_tokens(tokens), joined_in), TENSOR)
-    x = reshard(x_parts, z_count).astype(F32)
-
-    cut_gate = gate_up.astype(BF).reshape(rows, 2, 2, TP, UNITS).transpose(3, 1, 0, 2, 4)
-    cut_gate = after(cut_gate.reshape(TP, 2, rows, 2 * UNITS), x_parts)
-    cut_gate = exchange(cut_gate, TENSOR)
-    every_gate = lax.all_gather(cut_gate, SHARD, axis=0, tiled=False)
-    w_gate = to_full(every_gate, 2)
-
     def positions_of(order):
         base = (rank ^ jnp.array(order, jnp.int32)) * n
         quarters = (z_rank ^ jnp.arange(z_count, dtype=jnp.int32)) * z_tokens
@@ -471,6 +631,19 @@
     frequency = ROPE_BASE ** (-2.0 * jnp.arange(HEAD // 2, dtype=F32) / HEAD)
     angles = positions.astype(F32)[:, :, None] * frequency
     cosine, sine = jnp.cos(angles), jnp.sin(angles)
+    own_cosine, own_sine = jnp.where(core == 0, cosine, 1.0), jnp.where(core == 0, sine, 0.0)
+    cosine, sine, own_cosine, own_sine = (
+        after(table, x_parts) for table in (cosine, sine, own_cosine, own_sine)
+    )
+
+    cut_gate = cut_gate_up(gate_up, x_parts)
+    x = swap_z(x_parts.reshape(z_count, m * n, D))
+    x[-1] = after(x[-1], mixed_cols, cut_gate, cosine, sine, own_cosine, own_sine)
+    x = by_sequence(x, m).astype(F32)
+    cut_gate = exchange(cut_gate, TENSOR)
+    every_gate = lax.all_gather(cut_gate, SHARD, axis=0, tiled=False)
+    w_gate = to_full(every_gate, 2)
+
     prefixes = exchange(jnp.broadcast_to(prefix_lengths[None], (TP, seqs)), TENSOR).reshape(-1)
     prefixes = lax.dynamic_slice_in_dim(prefixes, z_rank * m, m)
     limit = jnp.maximum(positions, prefixes[:, None] - 1)[:, :, None]
@@ -478,66 +651,73 @@
 
     scale_one = rms_scale(x)
     normed_one = (x * scale_one * norm_gains[0]).astype(BF)
-    normed_one = gather_tokens(normed_one, middle=(joined,), end=(cut_gate,))
-    cut_down = exchange(after(down_proj.astype(BF).transpose(1, 0, 2), normed_one), TENSOR)
-    down_parts = exchange(after(share_tokens(cotangent), cut_gate), TENSOR)
-    mixed = dot(normed_one, w_mix).reshape(m, length, 2 * HEAD)
-    query = rotate(mixed[..., :HEAD], cosine, sine).astype(BF)
-    own = mixed[..., HEAD:]
-    own = jnp.where(core == 0, rotate(own, cosine, sine), own).astype(BF)
+    normed_one = gather_tokens(
+        normed_one, middle=(cut_gate,), end=(joined,)
+    )
+    low_down = down_proj.astype(BF).transpose(1, 0, 2)
+    parts = jnp.concatenate([low_down, share_tokens(cotangent).reshape(TP, seqs * n, D)], 1)
+    parts = exchange(after(parts, normed_one), TENSOR)
+    cut_down, down_parts = parts[:, :rows], parts[:, rows:]
+    flat = lambda table: table.reshape(m * length, HEAD // 2)
+    query, own = mix_forward(
+        normed_one, w_mix, flat(cosine), flat(sine), flat(own_cosine), flat(own_sine)
+    )
+    query, own = query.reshape(m, length, HEAD), own.reshape(m, length, HEAD)
     got = swap_halves(flip(own, "c"))
     key = jnp.where(core == 0, own, got)
     value = jnp.where(core == 0, got, own)
+    query = after(query, cut_down)
     attended, log_total = attend(limit, place, query, key, value)
-    attended = after(attended.reshape(m * length, HEAD), cut_down, down_parts)
-    down_in = reshard(after(down_parts, attended), z_count)
+    attended = attended.reshape(m * length, HEAD)
+    down_in = by_sequence(swap_z(after(down_parts, attended).reshape(z_count, m * n, D)), m)
     every_down = lax.all_gather(after(cut_down, every_gate), SHARD, axis=0, tiled=False)
     w_down = to_full(every_down, 1)
-    middle = x + scatter_tokens(attended, lambda part: dot(part, w_out))
+    middle = x + chip_sums(*core_sums(attended, lambda part: dot(part, w_out)))
     scale_two = rms_scale(middle)
     normed_two = (middle * scale_two * norm_gains[1]).astype(BF)
-    normed_two = gather_tokens(normed_two, middle=(down_in, every_gate))
+    normed_two = gather_tokens(normed_two, end=(every_gate, down_in))
     down_in = after(down_in, normed_two)
     hidden, gate_slope, up_slope = gate_forward(normed_two, w_gate)
 
-    def by_shard(grad, lead):
-        columns = grad.shape[-1]
-        grad = grad.reshape(lead, outer, TP, z_count, rows, columns).transpose(1, 3, 2, 0, 4, 5)
-        return grad.reshape(shards * TP * lead * rows, columns)
-
     def to_owners(grad):
+        grad = grad.reshape(-1, grad.shape[-1])
         return lax.psum_scatter(grad, SHARD, scatter_dimension=0, tiled=True)
 
+    grad_of = functools.partial(weight_grad, outer=outer, z_count=z_count, rows=rows)
     upstream = gather_tokens(down_in, middle=(hidden,))
-    g_down = by_shard(dot_tn(hidden, upstream, BF), 1)
+    g_down = grad_of(hidden, upstream)
     gate_rows = gate_back(after(upstream, g_down), w_down, gate_slope, up_slope)
-    g_gate_raw = dot_tn(normed_two, gate_rows, BF)
-    g_gate = by_shard(g_gate_raw, 2)
-    normed_grad = scatter_tokens(
-        gate_rows, lambda part: dot_nt(part, w_gate), middle=(g_gate_raw,), end=(g_gate,)
-    )
+    square = lambda w: w.astype(F32) * w.astype(F32)
+    own_in = jnp.sum(square(w_mix).reshape(2, B, 2, HEAD), (1, 3))
+    columns = jnp.stack([rank // 4, 2 + core])
+    own_in = jnp.zeros((2, 4), F32).at[:, columns].add(own_in).reshape(-1)
+    own_out = jnp.sum(square(w_out).reshape(HEAD, 2, B), (0, 2))
+    own_out = lax.dynamic_update_slice(jnp.zeros((2, 2), F32), own_out[None], (rank // 4, 0)).reshape(-1)
+    own_gate = jnp.sum(square(w_gate).reshape(2, B, 2, UNITS), (1, 3))[:, :, None]
+    own_gate = lax.dynamic_update_slice(jnp.zeros((2, 2, TP), F32), own_gate, (0, 0, rank)).reshape(-1)
+    own_down = jnp.sum(square(w_down).reshape(B, 2, B), (0, 2))
+    own_down = lax.dynamic_update_slice(jnp.zeros((TP, 2), F32), own_down[None], (rank, 0)).reshape(-1)
+    squares = jnp.concatenate([own_in, own_out, own_gate, own_down])
+    p, q = core_sums(gate_rows, lambda part: dot_nt(part, w_gate))
+    g_gate = grad_of(normed_two, gate_rows, others=(p, q))
+    normed_grad = chip_sums(p, q, middle=(g_gate,))
     middle_grad, gain_two = norm_back(middle, scale_two, norm_gains[1], normed_grad)
     middle_grad = middle_grad + down_in.astype(F32)
     g_down = to_owners(g_down)
     g_gate = to_owners(g_gate)
-    branch = gather_tokens(middle_grad.astype(BF), middle=(g_down,))
-    g_down = exchange(g_down.reshape(TP, 1, rows, D), TENSOR)
-    layer_out = middle + scatter_tokens(after(hidden, branch), lambda part: dot(part, w_down))
-    layer_output = reshard_back(layer_out.astype(BF), z_count, seqs)
+    p, q = core_sums(hidden, lambda part: dot(part, w_down))
+    branch = gather_tokens(middle_grad.astype(BF), middle=(g_down, p, q))
     attended_grad = dot_nt(branch, w_out, BF).reshape(m, length, HEAD)
-    query_grad, key_grad, value_grad = attend_back(
-        limit, place, query, key, value, log_total, attended_grad
-    )
-    keep = jnp.where(core == 0, key_grad, value_grad)
-    give = jnp.where(core == 0, value_grad, key_grad)
-    keep = keep + swap_halves(flip(give, "c"))
-    keep = jnp.where(core == 0, rotate(keep, cosine, -sine), keep)
-    mixed_grad = jnp.concatenate([rotate(query_grad, cosine, -sine), keep], -1).astype(BF)
+    query_grad, keep, give = attend_back(
+        core.reshape(1), limit, place, query, key, value, log_total, attended_grad, cosine, sine
+    )
+    mixed_grad = mix_back(query_grad, keep, flip(give, "c"), own_cosine, own_sine)
     mixed_grad = mixed_grad.reshape(m * length, 2 * HEAD)
 
-    g_mix = dot_tn(normed_one, mixed_grad, BF)
+    g_mix = grad_of(normed_one, mixed_grad)
+    layer_out = middle + chip_sums(p, q, start=(branch,), middle=(g_mix,))
+    g_down = exchange(after(g_down, g_mix).reshape(TP, 1, rows, D), TENSOR)
     g_out = dot_tn(attended, branch, BF)
-    g_mix = g_mix.reshape(2, outer, TP, z_count, rows, 2 * HEAD).transpose(1, 3, 2, 0, 4, 5)
     g_out = g_out.reshape(outer, 2, z_count, rows, 4, D // 4).transpose(0, 2, 4, 1, 3, 5)
     joined = jnp.concatenate(
         [
@@ -545,27 +725,34 @@
             g_out.reshape(shards, 8 * rows, D // 4),
         ],
         1,
-    ).reshape(shards * (mix_rows + 8 * rows), 2 * HEAD)
-    joined = to_owners(after(joined, g_gate, g_down))
+    )
+    joined = to_owners(after(joined, g_gate))
     g_gate = exchange(g_gate.reshape(TP, 2, rows, 2 * UNITS), TENSOR)
-    joined = after(joined, g_gate)
+    p, q = core_sums(mixed_grad, lambda part: dot_nt(part, w_mix))
+    normed_grad = chip_sums(p, q, start=(g_gate, layer_out))
+    layer_out = in_z_order(to_z(layer_out.astype(BF), m, z_count))
+    g_blocks = g_gate.reshape(TP, 2, rows, 2, UNITS).transpose(1, 3, 0, 2, 4).reshape(-1, rows, B)
+    d_blocks = g_down.reshape(TP, rows, 2, B).transpose(0, 2, 1, 3).reshape(-1, rows, B)
+    slots_here = left_stats.shape[0]
+    slots = jnp.arange(slots_here * devices, dtype=jnp.int32)
+    owner = (block_slots[None, :] == slots[:, None]).astype(BF)
+    early_blocks = jnp.concatenate([g_blocks, d_blocks], 0)
+    late = block_slots.shape[0] - early_blocks.shape[0]
+    place_blocks = lambda i, blocks, part: jnp.einsum(
+        "sb,bxy->sxy", owner[i::slots_here, part], blocks, preferred_element_type=F32
+    ).astype(BF)
+    early = [place_blocks(i, early_blocks, slice(late, None)) for i in range(slots_here)]
+    joined = after(joined, normed_grad, *early)
     g_mix = exchange(joined[:mix_rows].reshape(TP, 2, rows, 2 * HEAD), TENSOR)
     g_out = joined[mix_rows:].reshape(4, 2, rows, D // 4).transpose(1, 2, 0, 3).reshape(2, rows, D)
 
-    normed_grad = scatter_tokens(mixed_grad, lambda part: dot_nt(part, w_mix), end=(g_gate,))
     input_grad, gain_one = norm_back(x, scale_one, norm_gains[0], normed_grad)
+    weights = (attend_in, attend_out, gate_up, down_proj)
+    sums = sum_over(jnp.concatenate([gain_one, gain_two, squares]), TENSOR)
+    gains = gather_shards(sums[: 2 * D])
+    weight_size = STEP_RATE * jnp.sqrt(sums[2 * D :] / (B * B) + STEP_EPS)
     input_grad = input_grad + middle_grad
-    input_grad = after(input_grad.astype(BF), joined)
-    input_grad = reshard_back(input_grad, z_count, seqs).astype(F32)
-
-    weights = (attend_in, attend_out, gate_up, down_proj)
-    squares = [
-        jnp.sum((w * w).reshape(rows, w.shape[1], w.shape[2] // B, B), (0, 3)).reshape(-1)
-        for w in weights
-    ]
-    sums = sum_everywhere(jnp.concatenate([gain_one, gain_two] + squares))
-    gain_grads = sums[: 2 * D].reshape(2, D)
-    weight_size = STEP_RATE * jnp.sqrt(sums[2 * D :] / (B * B) + STEP_EPS)
+    input_grad = in_z_order(to_z(input_grad.astype(BF), m, z_count))
 
     g_heads = g_mix[..., :HEAD].transpose(2, 1, 0, 3).reshape(rows, 2, QD)
     g_kv = g_mix[..., HEAD:].reshape(KV_HEADS, 2, 2, rows, HEAD).transpose(3, 2, 1, 0, 4)
@@ -580,33 +767,36 @@
     )
     grad_down = g_down.reshape(TP, rows, D).transpose(1, 0, 2)
     grads = [grad_in, grad_out, grad_gate, grad_down]
+    wide_grads = [g.astype(F32) for g in grads]
 
     def to_blocks(array):
         k, columns = array.shape[1:]
         shaped = array.reshape(rows, k, columns // B, B).transpose(1, 2, 0, 3)
         return shaped.reshape(k * (columns // B), rows, B)
 
-    slots_here = left_stats.shape[0]
-    total_slots = slots_here * devices
-    owner = (block_slots[None, :] == jnp.arange(total_slots, dtype=jnp.int32)[:, None]).astype(BF)
-    g_blocks = g_gate.reshape(TP, 2, rows, 2, UNITS).transpose(1, 3, 0, 2, 4).reshape(-1, rows, B)
-    d_blocks = g_down.reshape(TP, rows, 2, B).transpose(0, 2, 1, 3).reshape(-1, rows, B)
-    grad_blocks = jnp.concatenate([to_blocks(grad_in), to_blocks(grad_out), g_blocks, d_blocks], 0)
-    product = lambda p, q: lax.dot_general(
-        p, q, (((1,), (0,)), ((), ())), preferred_element_type=F32
-    )
+    late_blocks = jnp.concatenate([to_blocks(grad_in), to_blocks(grad_out)], 0)
     returned, left_new, right_new = [], [], []
     for i in range(slots_here):
-        send = jnp.einsum(
-            "sb,bxy->sxy", owner[i::slots_here], grad_blocks, preferred_element_type=F32
-        ).astype(BF)
-        owned = exchange(send, ALL).reshape(B, B)
-        direction = dot(dot(left_roots[i].astype(BF), owned, BF), right_inverse_roots[i].astype(BF))
-        size = jnp.mean(direction * direction)
-        direction = (direction * lax.rsqrt(size + STEP_EPS)).astype(BF)
+        send = early[i] + place_blocks(i, late_blocks, slice(0, late))
+        if i == 1:
+            send = after(send, owned)
+        else:
+            send = after(send, input_grad, layer_out)
+        owned = exchange(send, ALL)
+        owned = owned.reshape(B, B)
+        direction = unit_direction(i, left_roots, right_inverse_roots, owned)
+        if i == 0:
+            direction = after(direction, weight_size, *wide_grads)
         returned.append(exchange(direction.reshape(devices, rows, B), ALL))
         left_new.append(STAT_DECAY * left_stats[i] + (1.0 - STAT_DECAY) * dot_nt(owned, owned))
         right_new.append(STAT_DECAY * right_stats[i] + (1.0 - STAT_DECAY) * dot_tn(owned, owned))
+    left_new, right_new = jnp.stack(left_new), jnp.stack(right_new)
+    returned[-1] = after(returned[-1], left_new, right_new)
+    tokens_back = [after(layer_out, returned[-1]), input_grad]
+    tokens_back = jnp.stack(tokens_back).reshape(2, TP, seqs, n, D)
+    tokens_back = exchange(tokens_back.transpose(1, 0, 2, 3, 4), TENSOR)
+    tokens_back = tokens_back.transpose(1, 2, 0, 3, 4).reshape(2, seqs, TP * n, D)
+    layer_output, input_grad = tokens_back[0], tokens_back[1].astype(F32)
     if slots_here == 1:
         returned = [returned[0][0::2], returned[0][1::2]]
     new_weights, offset = [], 0
@@ -615,15 +805,16 @@
         here = slice(offset, offset + count)
         new_weights.append(update(w, block_slots[here], weight_size[here], *returned))
         offset += count
+    gain_grads = sum_shards([after(part, new_weights[2]) for part in gains]).reshape(2, D)
     return (
         layer_output,
         input_grad,
-        *[g.astype(F32) for g in grads],
+        *wide_grads,
         gain_grads,
         *new_weights,
         norm_gains - GAIN_RATE * gain_grads,
-        jnp.stack(left_new),
-        jnp.stack(right_new),
+        left_new,
+        right_new,
     )
 
 

time: 1140 us -> 1100 us (0.965)
  Pallas kernels: 112 us -> 204 us
  matrix products: 179 us -> 103 us
  waiting for transfers between devices: 401 us -> 376 us
  starting transfers between devices: 151 us -> 132 us
    pallas_call x1 -> x9, Pallas kernels: 12.2 us -> 104 us  [the longest x3 48.1 us: weight_grad(): pl.pallas_call(weight_grad_kernel, grid=(features // tile,), in_specs=[pl...]
    dot_general x6 -> x3, matrix products: 54 us -> 17 us  [dot_tn(): lax.dot_general(x, y, (((0,), (0,)), ((), ())), preferred_element_type=F32)]
    dot_general x11 -> x8, matrix products: 59.2 us -> 23.1 us  [dot(): lax.dot_general(x, y, (((1,), (0,)), ((), ())), preferred_element_type=F32)]
    another operation x7 -> x3, other arithmetic: 35.2 us -> 8.51 us  [the longest x2 8.49 us: on_device(): left_new, right_new = (jnp.stack(left_new), jnp.stack(right_new))]
    ppermute x17 -> x18, waiting for transfers between devices: 81.3 us -> 57.9 us  [the longest x6 35.8 us: swap_z(): lax.ppermute(parts[i], 'z', [(j, j ^ i) for j in range(count)])]
    reshape x13 -> x6, local copies, waits for them, and re-layouts: 25.6 us -> 3.75 us  [the longest x1 3.31 us: on_device(): g_gate.reshape(TP, 2, rows, 2, UNITS).transpose(1, 3, 0, 2, 4)]
    all_gather x1, waiting for transfers between devices: 9.67 us -> 23.7 us  [on_device(): every_gate = lax.all_gather(cut_gate, SHARD, axis=0, tiled=False)]
    add x22, other arithmetic: 16.5 us -> 29.1 us  [the longest x2 11.5 us: on_device(): send = early[i] + place_blocks(i, late_blocks, slice(0, late))]
  transfers between devices with their start and end apart: 104 -> 103, of which waited for: 47 -> 45; matrix products, arithmetic and copies ran while one was open for 36% -> 28% of each run, Pallas kernels for 6% -> 19%
where the time goes in v3:
time: 1100 us; the launch traced here: 1090 us
  waiting for transfers between devices  376 us (34%)
  Pallas kernels  204 us (19%)
  local copies, waits for them, and re-layouts  159 us (14%)
  starting transfers between devices  132 us (12%)
  matrix products  103 us (9%)
  other arithmetic  99.1 us (9%)
  between operations  17.4 us (2%)
    ppermute x62, waiting for transfers between devices, flip(): return lax.ppermute(value, axis, [(0, 1), (1, 0)])  160 us
    all_to_all x13, waiting for transfers between devices, exchange(): return lax.all_to_all(value, axes, split_axis=0, concat_axis=0, tiled=True)  126 us
    dot_general x11, matrix products, dot_nt(): lax.dot_general(x, y, (((1,), (1,)), ((), ())), preferred_element_type=F32)  58.3 us
    all_to_all x13, starting transfers between devices, exchange(): return lax.all_to_all(value, axes, split_axis=0, concat_axis=0, tiled=True)  54.6 us
    unnamed x262, local copies, waits for them, and re-layouts  53.1 us
    pallas_call x3, Pallas kernels, weight_grad(): pl.pallas_call(weight_grad_kernel, grid=(features // tile,), in_specs=[pl...  48.1 us
    ppermute x62, starting transfers between devices, flip(): return lax.ppermute(value, axis, [(0, 1), (1, 0)])  43.3 us
    ppermute x6, waiting for transfers between devices, swap_z(): lax.ppermute(parts[i], 'z', [(j, j ^ i) for j in range(count)])  35.8 us
  transfers between devices with their start and end apart: 103, of which 45 were waited for; matrix products, arithmetic and copies ran while one was open for 28% of the time, Pallas kernels for 19%

profile of v3, /device:TPU:0, one launch (start us, length us, event | category | flops | bytes accessed | tf_op | source)
XLA Modules:
  0.0 1089.7 jit_solution(5476247915383629837)
XLA Ops:
  67.8 35.5 %collective-permute-done.1 = bf16[64,2048]{1,0:T(8,128)(2,1)} collective-permute-done((bf16[64,2048]{1,0:T(8,128)(2,1)}, bf16[64,2048]{1,0:T(8,128)(2,1)}, u32[]{:S(2)}, u32[]{:S(2)}) %collective-permute-start.1) | collective-permute-done | bytes 262176 | tf_op jit(solution)/shard_map/ppermute | solution.py:207
  118.6 19.7 %collective-permute-done.3.refs_1_ = bf16[256,2048]{1,0:T(8,128)(2,1)S(1)} collective-permute-done((bf16[256,2048]{1,0:T(8,128)(2,1)S(1)}, bf16[256,2048]{1,0:T(8,128)(2,1)S(1)}, u32[]{:S(2)}, u32[]{:S(2)}) %collective-permute-start.3) | collective-permute-done | bytes 1048608 | tf_op jit(solution)/shard_map/ppermute | solution.py:51
  181.9 10.4 mix_forward.1
  212.9 9.8 attend.1
  236.2 19.0 %collective-permute-done.16 = bf16[256,2048]{1,0:T(8,128)(2,1)} collective-permute-done((bf16[256,2048]{1,0:T(8,128)(2,1)}, bf16[256,2048]{1,0:T(8,128)(2,1)}, u32[]{:S(2)}, u32[]{:S(2)}) %collective-permute-start.16) | collective-permute-done | bytes 1048608 | tf_op jit(solution)/shard_map/ppermute | solution.py:51
  275.4 23.7 %all-gather.9.cloned.1.call-done = bf16[32,2,32,2048]{3,2,1,0:T(8,128)(2,1)} async-done(((bf16[8,2,32,2048]{3,2,1,0:T(8,128)(2,1)}), bf16[32,2,32,2048]{3,2,1,0:T(8,128)(2,1)}) %all-gather.9.cloned.1.call-update) | async-done | bytes 8388624 | tf_op jit(solution)/shard_map/all_gather | solution.py:644
  341.0 24.5 %gate_forward.1 = (bf16[2048,1024]{1,0:T(8,128)(2,1)S(1)}, f32[2048,1024]{1,0:T(8,128)}, f32[2048,1024]{1,0:T(8,128)}) custom-call(bf16[2048,2048]{1,0:T(8,128)(2,1)} %assemble.5.rows.refs_1_.left, bf16[2048,2048]{1,0:T(8,128)(2,1)} %bitcast.356), custom_call_target="tpu_custom_call" | custom-call | flops 17179869184 | bytes 37748736 | tf_op jit(solution)/shard_map/gate_forward/pallas_call | solution.py:484
  372.1 10.7 collective-permute-done.36.refs_3_
  391.7 13.7 %weight_grad.3.refs_1_ = bf16[1,4,8,1,32,2048]{5,4,3,2,1,0:T(8,128)(2,1)S(1)} custom-call(bf16[2048,1024]{1,0:T(8,128)(2,1)} %copy-done.14, bf16[2048,2048]{1,0:T(8,128)(2,1)} %assemble.6.right.refs_0_), custom_call_target="tpu_custom_call" | custom-call | flops 8589934592 | bytes 16777216 | tf_op jit(solution)/shard_map/weight_grad/pallas_call | solution.py:425
  410.7 18.3 %gate_back.1.right = bf16[2048,2048]{1,0:T(8,128)(2,1)} custom-call(bf16[2048,2048]{1,0:T(8,128)(2,1)} %after.57.rows, bf16[1024,2048]{1,0:T(8,128)(2,1)S(1)} %bitcast.299, f32[2048,1024]{1,0:T(8,128)} %get-tuple-element.28.gate_slope, f32[2048,1024]{1,0:T(8,128)} %get-tuple-element.29.up_slope), custom_call_target="tpu_custom_call" | custom-call | flops 8589934592 | bytes 37748736 | tf_op jit(solution)/shard_map/gate_back/pallas_call | solution.py:509
  458.6 24.5 %weight_grad.4.refs_1_ = bf16[1,4,8,2,32,2048]{5,4,3,2,1,0:T(8,128)(2,1)} custom-call(bf16[2048,2048]{1,0:T(8,128)(2,1)} %assemble.5.rows.refs_1_.left, bf16[2048,2048]{1,0:T(8,128)(2,1)} %gate_back.1.right, f32[512,2048]{1,0:T(8,128)S(1)} %convert_add_fusion.5.refs_0_, f32[512,2048]{1,0:T(8,128)} %convert_add_fusion.4.refs_1_), custom_call_target="tpu_custom_call" | custom-call | flops 17179869184 | bytes 25165824 | tf_op jit(solution)/shard_map/weight_grad/pallas_call | solution.py:425
  497.6 12.5 %collective-permute-done.44.refs_0_ = bf16[256,2048]{1,0:T(8,128)(2,1)S(1)} collective-permute-done((bf16[256,2048]{1,0:T(8,128)(2,1)S(1)}, bf16[256,2048]{1,0:T(8,128)(2,1)S(1)}, u32[]{:S(2)}, u32[]{:S(2)}) %collective-permute-start.44) | collective-permute-done | bytes 1048608 | tf_op jit(solution)/shard_map/ppermute | solution.py:51
  545.4 12.5 %collective-permute-done.50.refs_2_ = bf16[256,2048]{1,0:T(8,128)(2,1)S(1)} collective-permute-done((bf16[256,2048]{1,0:T(8,128)(2,1)S(1)}, bf16[256,2048]{1,0:T(8,128)(2,1)S(1)}, u32[]{:S(2)}, u32[]{:S(2)}) %collective-permute-start.50) | collective-permute-done | bytes 1048608 | tf_op jit(solution)/shard_map/ppermute | solution.py:51
  587.8 13.0 %attend_back.1 = (bf16[2,1024,256]{2,1,0:T(8,128)(2,1)S(1)}, f32[2,1024,256]{2,1,0:T(8,128)}, f32[2,1024,256]{2,1,0:T(8,128)}) custom-call(s32[1]{0:T(128)} %bitcast.50.core, s32[2,1024,1]{2,1,0:T(8,128)S(1)} %copy-done.44, s32[2,1,1024]{2,1,0:T(1,128)S(1)} %broadcast_in_dim.88.place, bf16[2,1024,256]{2,1,0:T(8,128)(2,1)S(1)} %copy-done.42, ...), custom_call_target="tpu_custom_call" | custom-call | flops 5368709120 | bytes 10485760 | tf_op jit(solution)/shard_map/attend_back/pallas_call | solution.py:319
  626.0 9.9 weight_grad.5.refs_1_
  720.1 11.8 %collective-permute-done.68 = bf16[256,2048]{1,0:T(8,128)(2,1)} collective-permute-done((bf16[256,2048]{1,0:T(8,128)(2,1)}, bf16[256,2048]{1,0:T(8,128)(2,1)}, u32[]{:S(2)}, u32[]{:S(2)}) %collective-permute-start.68) | collective-permute-done | bytes 1048608 | tf_op jit(solution)/shard_map/ppermute | solution.py:51
  738.0 9.3 collective-permute-done.69
  769.4 12.3 %collective-permute-done.76 = bf16[64,2048]{1,0:T(8,128)(2,1)S(1)} collective-permute-done((bf16[64,2048]{1,0:T(8,128)(2,1)S(1)}, bf16[64,2048]{1,0:T(8,128)(2,1)S(1)}, u32[]{:S(2)}, u32[]{:S(2)}) %collective-permute-start.76) | collective-permute-done | bytes 262176 | tf_op jit(solution)/shard_map/ppermute | solution.py:223
  831.1 39.5 %all-to-all-done.8 = bf16[32,32,1024]{2,1,0:T(8,128)(2,1)S(1)} async-done(((bf16[32,32,1024]{2,1,0:T(8,128)(2,1)}), bf16[32,32,1024]{2,1,0:T(8,128)(2,1)S(1)}, u32[]{:S(2)}, u32[]{:S(2)}) %all-to-all-start.8) | async-done | bytes 2097184 | tf_op jit(solution)/shard_map/all_to_all | solution.py:193
  898.6 25.0 %all-to-all-done.9 = bf16[32,32,1024]{2,1,0:T(8,128)(2,1)S(1)} async-done(((bf16[32,32,1024]{2,1,0:T(8,128)(2,1)}), bf16[32,32,1024]{2,1,0:T(8,128)(2,1)S(1)}, u32[]{:S(2)}, u32[]{:S(2)}) %all-to-all-start.9) | async-done | bytes 2097184 | tf_op jit(solution)/shard_map/all_to_all | solution.py:193
  923.6 10.1 unit_direction.2
  960.5 9.4 unit_direction.3.refs_0_
  1018.3 21.6 %all-to-all-done.12.refs_0_.refs_2_.refs_4_.refs_6_.refs_8_.refs_10_.refs_12_.refs_14_ = bf16[32,32,1024]{2,1,0:T(8,128)(2,1)} async-done(((bf16[32,32,1024]{2,1,0:T(8,128)(2,1)}), bf16[32,32,1024]{2,1,0:T(8,128)(2,1)}, u32[]{:S(2)}, u32[]{:S(2)}) %all-to-all-start.12) | async-done | bytes 2097184 | tf_op jit(solution)/shard_map/all_to_all | solution.py:193
  1049.6 11.8 %update.4.refs_1_ = f32[32,2,16384]{2,1,0:T(2,128)} custom-call(s32[32]{0:T(128)S(1)} %slice.531.slots, f32[32]{0:T(128)S(1)} %slice.533.sizes, f32[32,2,16384]{2,1,0:T(2,128)} %weight.4, bf16[32,32,1024]{2,1,0:T(8,128)(2,1)} %all-to-all-done.12.refs_0_.refs_2_.refs_4_.refs_6_.refs_8_.refs_10_.refs_12_.refs_14_, bf16[32,32,1024]{2,1,0:T(8,128)(2,1)S(1)} %copy-done.1, ...), custom_call_target="tpu_custom_call" | custom-call | tf_op jit(solution)/shard_map/update/pallas_call | solution.py:543
  (744 shorter events, 663.5 us)
Async XLA Ops:
  32.4 132.9 %all-gather.7.cloned.1.call-start = ((), (), s32[]{:S(2)}) async-start(), calls=%async_computation.19 | async-start | bytes 3932160 | tf_op jit(solution)/shard_map/all_gather | solution.py:618
  51.6 52.5 %collective-permute-start.2 = (bf16[64,2048]{1,0:T(8,128)(2,1)}, bf16[64,2048]{1,0:T(8,128)(2,1)S(1)}, u32[]{:S(2)}, u32[]{:S(2)}) collective-permute-start(bf16[64,2048]{1,0:T(8,128)(2,1)} %get-tuple-element.64), channel_id=1, source_target_pairs={{0,3},{1,2},{2,1},{3,0},{4,7},{5,6},{6,5},{7,4},{8,11},{9,10},{10,... | collective-permute-start | bytes 786440 | tf_op jit(solution)/shard_map/ppermute | solution.py:207
  54.1 49.1 %collective-permute-start.1 = (bf16[64,2048]{1,0:T(8,128)(2,1)}, bf16[64,2048]{1,0:T(8,128)(2,1)}, u32[]{:S(2)}, u32[]{:S(2)}) collective-permute-start(bf16[64,2048]{1,0:T(8,128)(2,1)} %get-tuple-element.65), channel_id=1, source_target_pairs={{0,2},{1,3},{2,0},{3,1},{4,6},{5,7},{6,4},{7,5},{8,10},{9,11},{10,... | collective-permute-start | bytes 786440 | tf_op jit(solution)/shard_map/ppermute | solution.py:207
  62.2 48.2 %all-to-all-start.3 = ((bf16[8,2,32,2048]{3,2,1,0:T(8,128)(2,1)}), bf16[8,2,32,2048]{3,2,1,0:T(8,128)(2,1)S(1)}, u32[]{:S(2)}, u32[]{:S(2)}) async-start(bf16[8,2,32,2048]{3,2,1,0:T(8,128)(2,1)} %cut_gate_up.1.refs_2_), calls=%async_computation.3 | async-start | bytes 4194304 | tf_op jit(solution)/shard_map/all_to_all | solution.py:193
  65.8 233.3 %all-gather.9.cloned.1.call-start = ((), (), s32[]{:S(2)}) async-start(), calls=%async_computation.20 | async-start | bytes 10485760 | tf_op jit(solution)/shard_map/all_gather | solution.py:644
  118.6 50.5 %collective-permute-start.6 = (bf16[256,2048]{1,0:T(8,128)(2,1)S(1)}, bf16[256,2048]{1,0:T(8,128)(2,1)}, u32[]{:S(2)}, u32[]{:S(2)}) collective-permute-start(bf16[256,2048]{1,0:T(8,128)(2,1)S(1)} %fusion.12.refs_0_), channel_id=1, source_target_pairs={{0,4},{4,0},{1,5},{5,1},{2,6},{6,2},{3,7},{7,3},{8,12},{12,8},{9,1... | collective-permute-start | bytes 3145736 | tf_op jit(solution)/shard_map/ppermute | solution.py:51
  211.7 196.1 %all-gather.11.cloned.1.call-start = ((), (), s32[]{:S(2)}) async-start(), calls=%async_computation.21 | async-start | bytes 5242880 | tf_op jit(solution)/shard_map/all_gather | solution.py:673
  261.1 40.5 %collective-permute-start.30 = (bf16[64,2048]{1,0:T(8,128)(2,1)S(1)}, bf16[64,2048]{1,0:T(8,128)(2,1)}, u32[]{:S(2)}, u32[]{:S(2)}) collective-permute-start(bf16[64,2048]{1,0:T(8,128)(2,1)S(1)} %get-tuple-element.59), channel_id=1, source_target_pairs={{0,3},{1,2},{2,1},{3,0},{4,7},{5,6},{6,5},{7,4},{8,11},{9,10},{10,... | collective-permute-start | bytes 786440 | tf_op jit(solution)/shard_map/ppermute | solution.py:207
  264.3 36.3 %collective-permute-start.29 = (bf16[64,2048]{1,0:T(8,128)(2,1)}, bf16[64,2048]{1,0:T(8,128)(2,1)}, u32[]{:S(2)}, u32[]{:S(2)}) collective-permute-start(bf16[64,2048]{1,0:T(8,128)(2,1)} %get-tuple-element.60), channel_id=1, source_target_pairs={{0,2},{1,3},{2,0},{3,1},{4,6},{5,7},{6,4},{7,5},{8,10},{9,11},{10,... | collective-permute-start | bytes 786440 | tf_op jit(solution)/shard_map/ppermute | solution.py:207
  264.3 35.1 %collective-permute-start.28 = (bf16[64,2048]{1,0:T(8,128)(2,1)}, bf16[64,2048]{1,0:T(8,128)(2,1)}, u32[]{:S(2)}, u32[]{:S(2)}) collective-permute-start(bf16[64,2048]{1,0:T(8,128)(2,1)} %get-tuple-element.61), channel_id=1, source_target_pairs={{0,1},{1,0},{2,3},{3,2},{4,5},{5,4},{6,7},{7,6},{8,9},{9,8},{10,11... | collective-permute-start | bytes 786440 | tf_op jit(solution)/shard_map/ppermute | solution.py:207
  299.2 259.5 %reduce-scatter.4.cloned.1.call-start = ((), (), s32[]{:S(2)}) async-start(), calls=%async_computation.16 | async-start | bytes 5242880 | tf_op jit(solution)/shard_map/reduce_scatter | solution.py:684
  330.4 54.0 %collective-permute-start.37 = (bf16[256,2048]{1,0:T(8,128)(2,1)}, bf16[256,2048]{1,0:T(8,128)(2,1)}, u32[]{:S(2)}, u32[]{:S(2)}) collective-permute-start(bf16[256,2048]{1,0:T(8,128)(2,1)} %after.54.refs_0_), channel_id=1, source_target_pairs={{0,4},{4,0},{1,5},{5,1},{2,6},{6,2},{3,7},{7,3},{8,12},{12,8},{9,1... | collective-permute-start | bytes 3145736 | tf_op jit(solution)/shard_map/ppermute | solution.py:51
  331.0 36.5 %collective-permute-start.35 = (bf16[256,2048]{1,0:T(8,128)(2,1)}, bf16[256,2048]{1,0:T(8,128)(2,1)S(1)}, u32[]{:S(2)}, u32[]{:S(2)}) collective-permute-start(bf16[256,2048]{1,0:T(8,128)(2,1)} %after.54.refs_0_), channel_id=1, source_target_pairs={{0,16},{16,0},{1,17},{17,1},{2,18},{18,2},{3,19},{19,3},{4,20},{20... | collective-permute-start | bytes 3145736 | tf_op jit(solution)/shard_map/ppermute | solution.py:51
  332.4 36.0 %collective-permute-start.34 = (bf16[256,2048]{1,0:T(8,128)(2,1)}, bf16[256,2048]{1,0:T(8,128)(2,1)S(1)}, u32[]{:S(2)}, u32[]{:S(2)}) collective-permute-start(bf16[256,2048]{1,0:T(8,128)(2,1)} %after.54.refs_0_), channel_id=1, source_target_pairs={{0,8},{8,0},{1,9},{9,1},{2,10},{10,2},{3,11},{11,3},{4,12},{12,4},... | collective-permute-start | bytes 3145736 | tf_op jit(solution)/shard_map/ppermute | solution.py:51
  407.5 252.3 %reduce-scatter.6.cloned.1.call-start = ((), (), s32[]{:S(2)}) async-start(), calls=%async_computation.17 | async-start | bytes 10485760 | tf_op jit(solution)/shard_map/reduce_scatter | solution.py:684
  651.2 45.7 %collective-permute-start.70 = (bf16[512,2048]{1,0:T(8,128)(2,1)}, bf16[512,2048]{1,0:T(8,128)(2,1)}, u32[]{:S(2)}, u32[]{:S(2)}) collective-permute-start(bf16[512,2048]{1,0:T(8,128)(2,1)} %convolution_convert_fusion.4), channel_id=1, source_target_pairs={{0,4},{4,0},{1,5},{5,1},{2,6},{6,2},{3,7},{7,3},{8,12},{12,8},{9,1... | collective-permute-start | bytes 6291464 | tf_op jit(solution)/shard_map/ppermute | solution.py:51
  695.0 86.7 %reduce-scatter.8.cloned.1.call-start = ((), (), s32[]{:S(2)}) async-start(), calls=%async_computation.18 | async-start | bytes 3932160 | tf_op jit(solution)/shard_map/reduce_scatter | solution.py:684
  695.1 36.9 %collective-permute-start.68 = (bf16[256,2048]{1,0:T(8,128)(2,1)}, bf16[256,2048]{1,0:T(8,128)(2,1)}, u32[]{:S(2)}, u32[]{:S(2)}) collective-permute-start(bf16[256,2048]{1,0:T(8,128)(2,1)} %after.68), channel_id=1, source_target_pairs={{0,16},{16,0},{1,17},{17,1},{2,18},{18,2},{3,19},{19,3},{4,20},{20... | collective-permute-start | bytes 3145736 | tf_op jit(solution)/shard_map/ppermute | solution.py:51
  819.6 51.1 %all-to-all-start.8 = ((bf16[32,32,1024]{2,1,0:T(8,128)(2,1)}), bf16[32,32,1024]{2,1,0:T(8,128)(2,1)S(1)}, u32[]{:S(2)}, u32[]{:S(2)}) async-start(bf16[32,32,1024]{2,1,0:T(8,128)(2,1)} %after.71), calls=%async_computation.11 | async-start | bytes 4194304 | tf_op jit(solution)/shard_map/all_to_all | solution.py:193
  872.0 51.7 %all-to-all-start.9 = ((bf16[32,32,1024]{2,1,0:T(8,128)(2,1)}), bf16[32,32,1024]{2,1,0:T(8,128)(2,1)S(1)}, u32[]{:S(2)}, u32[]{:S(2)}) async-start(bf16[32,32,1024]{2,1,0:T(8,128)(2,1)} %after.72), calls=%async_computation.12 | async-start | bytes 4194304 | tf_op jit(solution)/shard_map/all_to_all | solution.py:193
  895.2 47.4 %collective-permute-start.79 = (f32[4156]{0:T(1024)S(1)}, f32[4156]{0:T(1024)S(1)}, u32[]{:S(2)}, u32[]{:S(2)}) collective-permute-start(f32[4156]{0:T(1024)S(1)} %add.401), channel_id=1, source_target_pairs={{0,8},{8,0},{1,9},{9,1},{2,10},{10,2},{3,11},{11,3},{4,12},{12,4},... | collective-permute-start | bytes 49880 | tf_op jit(solution)/shard_map/ppermute | solution.py:158
  935.1 51.7 %all-to-all-start.10 = ((bf16[32,32,1024]{2,1,0:T(8,128)(2,1)}), bf16[32,32,1024]{2,1,0:T(8,128)(2,1)S(1)}, u32[]{:S(2)}, u32[]{:S(2)}) async-start(bf16[32,32,1024]{2,1,0:T(8,128)(2,1)} %bitcast.314), calls=%async_computation.13 | async-start | bytes 4194304 | tf_op jit(solution)/shard_map/all_to_all | solution.py:193
  988.2 51.8 %all-to-all-start.12 = ((bf16[32,32,1024]{2,1,0:T(8,128)(2,1)}), bf16[32,32,1024]{2,1,0:T(8,128)(2,1)}, u32[]{:S(2)}, u32[]{:S(2)}) async-start(bf16[32,32,1024]{2,1,0:T(8,128)(2,1)} %bitcast.295), calls=%async_computation.15 | async-start | bytes 4194304 | tf_op jit(solution)/shard_map/all_to_all | solution.py:193
  1040.0 38.5 %all-to-all-start.11 = ((bf16[8,2,1,32,2048]{4,3,2,1,0:T(8,128)(2,1)}), bf16[8,2,1,32,2048]{4,3,2,1,0:T(8,128)(2,1)}, u32[]{:S(2)}, u32[]{:S(2)}) async-start(bf16[8,2,1,32,2048]{4,3,2,1,0:T(8,128)(2,1)} %maximum_bitcast_fusion), calls=%async_computation.14 | async-start | bytes 4194304 | tf_op jit(solution)/shard_map/all_to_all | solution.py:193
  (200 other events, 2425.4 us)
Sparse Core Ops, SparseCore 0:
  43.3 82.5 all-gather.6
  128.0 171.0 all-gather.8
  300.7 79.7 all-gather.10
  407.6 75.0 reduce-scatter.3
  485.0 144.9 reduce-scatter.5
  703.7 61.7 reduce-scatter.7
